TPU v7x, 128 devices: a whole 4x4x4 slice. The times are simulated.
128 devices in a mesh: region: 4 (over x), wave: 32 (over y, z, core).
Axes of the slice: x: 4, y: 4, z: 4, core: 2. Of those that a mesh axis runs over, the one named last changes fastest.
Arguments:
- state0: float32 [9, 35, 32768], P(None, None, ('region', 'wave')), may hold values from -6 to 6
- delta: float32 [9, 35, 32768], P(None, None, ('region', 'wave')), may hold values from -6 to 6
- adjoint: float32 [9, 35, 32768], P(None, None, ('region', 'wave')), may hold values from -6 to 6
- model: float32 [3, 35, 32768], P(None, None, ('region', 'wave')), may hold values from 0.5 to 2
- geometry: float32 [9, 32768], P(None, ('region', 'wave')), may hold values from -4 to 4
- normals: float32 [3, 4, 32768], P(None, None, ('region', 'wave')), may hold values from -1 to 1
- face_scale: float32 [4, 32768], P(None, ('region', 'wave')), may hold values from 0.5 to 2
- derivative: float32 [3, 35, 35], replicated, may hold values from -1 to 1
- lift: float32 [4, 35, 15], replicated, may hold values from -1.5 to 1.5
- prolong: float32 [8, 35, 10], replicated, may hold values from -2 to 2
- coarse_step: float32 [30, 4096], P(None, ('region', 'wave')), may hold values from -6 to 6
- reg_weight: float32 [30, 4096], P(None, ('region', 'wave')), may hold values from 1 to 10
- observe: float32 [35, 32768], P(None, ('region', 'wave')), may hold values from 0.1 to 1
- owner: int32 [32768, 1], P(('region', 'wave')), may hold values from 0 to 127; in each aligned block of 256 rows (0 to 255, 256 to 511, ...) at most 4 rows name the same one
- coarse_local: int32 [32768], P(('region', 'wave')), may hold values from 0 to 31
- child: int32 [32768], P(('region', 'wave')), may hold values from 0 to 7
- neighbor: int32 [4, 32768], P(None, ('region', 'wave')), may hold values from 0 to 1151
- orient: int32 [4, 32768], P(None, ('region', 'wave')), may hold values from 0 to 5
- send_face: int32 [16384], P(('region', 'wave')), may hold values from 0 to 1023
Outputs:
- delta_next: float32 [9, 35, 32768], P(None, None, ('region', 'wave'))
- adjoint_next: float32 [9, 35, 32768], P(None, None, ('region', 'wave'))
- hess_vec: float32 [30, 4096], P(None, ('region', 'wave'))
Inputs may be any that keep to these rules, and one draw needn't show every extreme that they name: `owner`: no more than 4 fine elements of one device have coarse elements owned by one device, and that number is reached. `send_face`: entries w * 4 to w * 4 + 3 of a device name its traces for wave partition w.
All inputs are finite; a program needn't handle non-finite values.
Results may differ from a plain program's by a relative error of at most 0.0003.
Values sent between devices are 32-bit elements; how exact they have to be, the bound alone decides.
A program may use at most 128 MiB of HBM per device.

v0:
```python
import functools

import jax
import jax.numpy as jnp
import numpy as np
from jax import lax
from jax.experimental import pallas as pl
from jax.experimental.pallas import tpu as pltpu
from jax.sharding import PartitionSpec as P

f32, bf16, i32, i16 = jnp.float32, jnp.bfloat16, jnp.int32, jnp.int16
MESH = pl.DeviceIdType.MESH

STEP = 0.2
STRESS = ((0, 5, 4), (5, 1, 3), (4, 3, 2))
OFF = ((1, 2), (0, 2), (0, 1))
NF, NN, E, NW, ND = 9, 35, 256, 32, 128
OWN, TAB = 1024, 1152
ROWS = 27 * 16


def tables():
    triangle = [(a, b) for a in range(5) for b in range(5 - a)]
    nodes = [(a, b, c) for a in range(5) for b in range(5 - a) for c in range(5 - a - b)]
    face = np.zeros((4, 15), np.int32)
    for at, (a, b) in enumerate(triangle):
        for f, key in enumerate(((a, b, 0), (a, 0, b), (0, a, b), (a, b, 4 - a - b))):
            face[f, at] = nodes.index(key)
    orders = [(0, 1, 2), (1, 2, 0), (2, 0, 1), (0, 2, 1), (2, 1, 0), (1, 0, 2)]
    turning = np.zeros((6, 15), np.int32)
    for o, order in enumerate(orders):
        for at, (a, b) in enumerate(triangle):
            triple = (a, b, 4 - a - b)
            turning[o, at] = triangle.index((triple[order[0]], triple[order[1]]))
    return face, turning


def constants():
    face, turning = tables()
    pick = np.zeros((128, 144), np.float32)
    for f in range(4):
        for m in range(15):
            pick[f * 16 + m, face[f, m]] = 1.0
            pick[64 + f * 16 + m, 48 + face[f, m]] = 1.0
    turn = np.full((16, 128), 15, np.int32)
    for o in range(6):
        turn[:15, o] = turning[o]
    return pick, turn


def split(x):
    hi = x.astype(bf16)
    lo = (x - hi.astype(f32)).astype(bf16)
    return hi, lo


def nn(a, b):
    return lax.dot_general(a, b, (((1,), (0,)), ((), ())), preferred_element_type=f32)


def nt(a, b):
    return lax.dot_general(a, b, (((1,), (1,)), ((), ())), preferred_element_type=f32)


def tn(a, b):
    return lax.dot_general(a, b, (((0,), (0,)), ((), ())), preferred_element_type=f32)


def iota(shape, dim, kind=i32):
    return lax.broadcasted_iota(kind, shape, dim)


def below(x, rows):
    return jnp.concatenate([x, jnp.zeros((rows - x.shape[0], x.shape[1]), x.dtype)], axis=0)


def lanes3(x, width):
    hi = x.astype(bf16).astype(f32)
    lo = x - hi
    zero = jnp.zeros((x.shape[0], width - x.shape[1]), f32)
    return jnp.concatenate([hi, zero, hi, zero, lo, zero], axis=1).astype(bf16)


def rows3(x):
    hi, lo = split(x)
    return jnp.concatenate([hi, lo, hi], axis=0)


def kernel(
    s0, dl, ad, model, geometry, normals, face_scale, derivative, lift, prolong, coarse, reg, observe,
    owner, local, child, neighbor, orient, send_face, pick, turn,
    out_d, out_a, out_h,
    tab, hot, dq, jump, hn, xl, fs, ltr, rst, c1,
    tr_s, tr_r, rq_s, rq_r, an_s, an_r, pt_s, pt_r,
    ssem, rsem,
):
    region, wave = lax.axis_index("region"), lax.axis_index("wave")
    me = region * NW + wave
    barrier = pltpu.get_barrier_semaphore()

    def where_is(i):
        d = lax.rem(me + i, ND)
        return d, (lax.div(d, NW), lax.rem(d, NW))

    def greet(i, c):
        pl.semaphore_signal(barrier, inc=1, device_id=where_is(i)[1], device_id_type=MESH)
        return c

    lax.fori_loop(1, ND, greet, 0)

    def send_rows(src, dst, at):
        def one(i, c):
            d, there = where_is(i)
            pltpu.make_async_remote_copy(
                src_ref=src.at[d], dst_ref=dst.at[me], send_sem=ssem.at[at], recv_sem=rsem.at[at],
                device_id=there, device_id_type=MESH,
            ).start()
            return c

        lax.fori_loop(1, ND, one, 0)
        dst[pl.ds(me, 1)] = src[pl.ds(me, 1)]

    def wait_rows(ref, sem):
        part = ref.at[pl.ds(0, ND - 1)]
        pltpu.make_async_copy(part, part, sem).wait()

    u = (iota((ND, E), 0) == owner[...]).astype(f32).astype(bf16)
    ub = u.astype(f32)
    tri = (iota((E, E), 0) < iota((E, E), 1)).astype(f32).astype(bf16)
    before = jnp.sum(nn(u, tri) * ub, axis=0, keepdims=True).astype(i32)
    code = before * 32 + local[...]
    vt = (iota((128, E), 0) == code).astype(f32).astype(bf16)
    rq_s.reshape(ND, 128)[...] = nt(u, vt)

    for k in range(3):
        c1[k * 40:(k + 1) * 40, :] = lanes3(below(derivative[k], 40), 48)
    c1[120:248, :] = pick[...]
    for s, ref in enumerate((s0, dl, ad)):
        for c in range(NF):
            sc = s * NF + c
            got = nn(c1[...], rows3(below(ref[c], 48)))
            dq[sc] = got[0:120]
            for f in range(4):
                span = slice(f * E, (f + 1) * E)
                tab[0, sc * 16:(sc + 1) * 16, span] = got[120 + f * 16:136 + f * 16].astype(bf16)
                tab[1, sc * 16:(sc + 1) * 16, span] = got[184 + f * 16:200 + f * 16].astype(bf16)

    pickt = (iota((OWN, 128), 0) == send_face[...]).astype(f32).astype(bf16)
    sent = nn(tab[0, :, 0:OWN], pickt) + nn(tab[1, :, 0:OWN], pickt)
    sent = below(sent, 512)
    for j in range(4):
        tr_s.reshape(4, 128, 128)[j] = sent[j * 128:(j + 1) * 128].T

    pl.semaphore_wait(barrier, ND - 1)
    send_rows(rq_s, rq_r, 0)

    def send_trace(i, c):
        w = lax.rem(wave + i, NW)
        pltpu.make_async_remote_copy(
            src_ref=tr_s.at[:, pl.ds(w, 1)], dst_ref=tr_r.at[:, pl.ds(wave, 1)],
            send_sem=ssem.at[1], recv_sem=rsem.at[1], device_id=(region, w), device_id_type=MESH,
        ).start()
        return c

    lax.fori_loop(1, NW, send_trace, 0)
    tr_r[:, pl.ds(wave, 1)] = tr_s[:, pl.ds(wave, 1)]

    for f in range(4):
        row = neighbor[f:f + 1, :].astype(i16)
        hot[:, f * E:(f + 1) * E] = jnp.where(
            iota((TAB, E), 0, i16) == row, jnp.ones((), bf16), jnp.zeros((), bf16)
        )

    wait_rows(rq_r, rsem.at[0])
    asked = rq_r.reshape(ND, 128)[...].astype(bf16)
    cs = jnp.concatenate([coarse[...], jnp.zeros((2, 32), f32)], axis=0)
    cs4 = jnp.concatenate([cs] * 4, axis=1)
    cs16 = jnp.concatenate([cs4] * 4, axis=0)
    same = lax.div(iota((128, 128), 0), 32) == lax.div(iota((128, 128), 1), 32)
    bh, bl = split(jnp.where(same, cs16, 0.0))
    an_s.reshape(ND, 128)[...] = nt(asked, bh) + nt(asked, bl)
    send_rows(an_s, an_r, 2)

    for f in range(4):
        span = slice(f * E, (f + 1) * E)
        jump[:, span] = nn(tab[0, :, 0:OWN], hot[0:OWN, span]) + nn(tab[1, :, 0:OWN], hot[0:OWN, span])

    part = tr_r.at[:, pl.ds(0, NW - 1)]
    pltpu.make_async_copy(part, part, rsem.at[1]).wait()
    for j in range(4):
        rows = min(128, ROWS - j * 128)
        hi, lo = split(tr_r.reshape(4, 128, 128)[j].T[0:rows])
        tab[0, j * 128:j * 128 + rows, OWN:TAB] = hi
        tab[1, j * 128:j * 128 + rows, OWN:TAB] = lo
    for f in range(4):
        span = slice(f * E, (f + 1) * E)
        jump[:, span] += nn(tab[0, :, OWN:TAB], hot[OWN:TAB, span]) + nn(tab[1, :, OWN:TAB], hot[OWN:TAB, span])

    for f in range(4):
        span = slice(f * E, (f + 1) * E)
        h = 0.5 * face_scale[f:f + 1, :]
        for j in range(3):
            hn[j, :, span] = jnp.broadcast_to(h * normals[j, f:f + 1, :], (8, E))
        hn[3, :, span] = jnp.broadcast_to(h, (8, E))

    ltr[...] = jnp.zeros_like(ltr)
    for f in range(4):
        for m in range(15):
            ltr[f * 16 + m:f * 16 + m + 1, 0:NN] = lift[m, f:f + 1, :]
    lh, ll = split(ltr[...].T[0:40])
    lmat = jnp.concatenate([lh.astype(f32), lh.astype(f32), ll.astype(f32)], axis=1).astype(bf16)

    for f in range(4):
        span = slice(f * E, (f + 1) * E)
        o = orient[f:f + 1, :]
        idx = jnp.full((16, E), 15, i32)
        for q in range(6):
            idx = jnp.where(o == q, turn[:, q:q + 1], idx)
        low = idx < 8
        idx = idx & 7
        ia, ib = idx[0:8], idx[8:16]
        for sc in range(27):
            a = jump[sc * 16:sc * 16 + 8, span]
            b = jump[sc * 16 + 8:sc * 16 + 16, span]
            own = tab[0, sc * 16:sc * 16 + 16, span].astype(f32) + tab[1, sc * 16:sc * 16 + 16, span].astype(f32)
            for t, ix in enumerate((ia, ib)):
                ga = jnp.take_along_axis(a, ix, axis=0, mode="promise_in_bounds")
                gb = jnp.take_along_axis(b, ix, axis=0, mode="promise_in_bounds")
                jump[sc * 16 + t * 8:sc * 16 + t * 8 + 8, span] = (
                    jnp.where(low[t * 8:t * 8 + 8], ga, gb) - own[t * 8:t * 8 + 8]
                )

    geo = [geometry[q:q + 1, :] for q in range(9)]

    def grad(sc, i):
        return sum(geo[3 * i + k] * dq[sc, k * 40:(k + 1) * 40, :] for k in range(3))

    for s in range(3):
        for f in range(4):
            span = slice(f * E, (f + 1) * E)
            n = [jnp.concatenate([hn[j, :, span]] * 2, axis=0) for j in range(4)]
            q = [jump[(s * NF + c) * 16:(s * NF + c) * 16 + 16, span] for c in range(NF)]
            chans = [sum(n[j] * q[3 + STRESS[i][j]] for j in range(3)) for i in range(3)]
            chans += [n[j] * q[j] for j in range(3)]
            chans += [n[i] * q[j] + n[j] * q[i] for i, j in OFF]
            if s > 0:
                chans += [n[3] * q[c] for c in range(NF)]
            for at, g in enumerate(chans):
                hi, lo = split(g)
                xl[at, f * 16:f * 16 + 16, :] = hi
                xl[at, 64 + f * 16:80 + f * 16, :] = lo
                xl[at, 128 + f * 16:144 + f * 16, :] = hi
        base = s * NF
        for i in range(3):
            fs[s, i] = nn(lmat, xl[i]) + sum(grad(base + 3 + STRESS[i][j], j) for j in range(3))
            fs[s, 3 + i] = nn(lmat, xl[3 + i]) + grad(base + i, i)
        for at, (i, j) in enumerate(OFF):
            fs[s, 6 + at] = nn(lmat, xl[6 + at]) + grad(base + j, i) + grad(base + i, j)
        if s > 0:
            for c in range(NF):
                fs[s, 9 + c] = nn(lmat, xl[9 + c])

    wait_rows(an_r, rsem.at[2])
    ah, al = split(an_r.reshape(ND, 128)[...])
    slot = lax.div(iota((128, E), 0), 32) == before
    found = jnp.where(slot, tn(ah, u) + tn(al, u), 0.0)
    found = found[0:32] + found[32:64] + found[64:96] + found[96:128]
    mask = (iota((8, E), 0) == child[...]).astype(f32)
    pm = prolong[...].reshape(80, NN)
    pm40 = jnp.concatenate([pm, jnp.zeros((80, 5), f32)], axis=1)
    ph, pw = split(pm40)
    pm3 = jnp.concatenate([ph, ph, pw], axis=0)
    fine = []
    for p in range(3):
        z = jnp.concatenate([mask * found[p * 10 + k:p * 10 + k + 1, :] for k in range(10)], axis=0)
        fine.append(tn(pm3, rows3(z)))

    m0, m1, m2 = (below(model[p], 40) for p in range(3))

    def lam(s):
        return fs[s, 3] + fs[s, 4] + fs[s, 5]

    def mu(s, k):
        return 2.0 * fs[s, 3 + k] if k < 3 else fs[s, 3 + k]

    lam0 = lam(0)
    lam1 = m1 * lam(1) + fine[1] * lam0
    lam2 = m1 * lam(2)
    obs = below(observe[...], 40)
    gb = jnp.zeros((40, E), f32)
    tr = jnp.zeros((40, E), f32)
    gm = jnp.zeros((40, E), f32)
    for c in range(NF):
        if c < 3:
            wave_d = m0 * fs[1, c] + fine[0] * fs[0, c]
            wave_a = m0 * fs[2, c]
        else:
            wave_d = m2 * mu(1, c - 3) + fine[2] * mu(0, c - 3)
            wave_a = m2 * mu(2, c - 3)
            if c < 6:
                wave_d = wave_d + lam1
                wave_a = wave_a + lam2
        nd = below(dl[c], 40) + STEP * (wave_d + fs[1, 9 + c])
        na = below(ad[c], 40) + STEP * (wave_a + fs[2, 9 + c] + obs * nd)
        out_d[c] = nd[0:NN]
        out_a[c] = na[0:NN]
        if c < 3:
            gb = gb + na * fs[0, c]
        else:
            gm = gm + na * mu(0, c - 3)
            if c < 6:
                tr = tr + na
    fine_grad = (STEP * gb, STEP * tr * lam0, STEP * gm)

    pm144 = lanes3(pm, 48)
    rst[...] = jnp.zeros_like(rst)
    for p in range(3):
        r = nn(pm144, rows3(below(fine_grad[p], 48)))
        rst[p * 10:(p + 1) * 10, :] = jnp.sum(r.reshape(10, 8, E) * mask[None], axis=1)
    wh, wl = split(jnp.where(slot, jnp.concatenate([rst[...]] * 4, axis=0), 0.0))
    pt_s.reshape(ND, 128)[...] = nt(u, wh) + nt(u, wl)
    send_rows(pt_s, pt_r, 3)
    wait_rows(pt_r, rsem.at[3])
    gh, gl = split(pt_r.reshape(ND, 128)[...])
    total = jnp.where(same, tn(gh, asked) + tn(gl, asked), 0.0)
    total = total[0:32] + total[32:64] + total[64:96] + total[96:128]
    total = total[:, 0:32] + total[:, 32:64] + total[:, 64:96] + total[:, 96:128]
    out_h[...] = total[0:30] + reg[...] * coarse[...]

    wait_rows(rq_s, ssem.at[0])
    part = tr_s.at[:, pl.ds(0, NW - 1)]
    pltpu.make_async_copy(part, part, ssem.at[1]).wait()
    wait_rows(an_s, ssem.at[2])
    wait_rows(pt_s, ssem.at[3])


def body(
    state0, delta, adjoint, model, geometry, normals, face_scale, derivative, lift, prolong, coarse_step, reg_weight,
    observe, owner, coarse_local, child, neighbor, orient, send_face,
):
    pick, turn = constants()
    ops = (
        state0, delta, adjoint, model, geometry, normals, face_scale, derivative,
        lift.transpose(2, 0, 1), prolong.transpose(2, 0, 1), coarse_step, reg_weight, observe,
        owner.reshape(1, E), coarse_local.reshape(1, E), child.reshape(1, E), neighbor, orient, send_face.reshape(1, 128),
        jnp.asarray(pick, bf16), jnp.asarray(turn),
    )
    vmem = pl.BlockSpec(memory_space=pltpu.VMEM)
    row = pltpu.VMEM((ND, 1, 128), f32)
    return pl.pallas_call(
        kernel,
        out_shape=(
            jax.ShapeDtypeStruct((NF, NN, E), f32),
            jax.ShapeDtypeStruct((NF, NN, E), f32),
            jax.ShapeDtypeStruct((30, 32), f32),
        ),
        in_specs=[vmem] * len(ops),
        out_specs=(vmem, vmem, vmem),
        scratch_shapes=[
            pltpu.VMEM((2, ROWS, TAB), bf16),
            pltpu.VMEM((TAB, OWN), bf16),
            pltpu.VMEM((27, 120, E), f32),
            pltpu.VMEM((ROWS, OWN), f32),
            pltpu.VMEM((4, 8, OWN), f32),
            pltpu.VMEM((18, 192, E), bf16),
            pltpu.VMEM((3, 18, 40, E), f32),
            pltpu.VMEM((64, 128), f32),
            pltpu.VMEM((32, E), f32),
            pltpu.VMEM((248, 144), bf16),
            pltpu.VMEM((4, NW, 4, 128), f32),
            pltpu.VMEM((4, NW, 4, 128), f32),
            row, row, row, row, row, row,
            pltpu.SemaphoreType.DMA((4,)),
            pltpu.SemaphoreType.DMA((4,)),
        ],
        compiler_params=pltpu.CompilerParams(
            collective_id=0, has_side_effects=True, vmem_limit_bytes=48 * 1024 * 1024
        ),
    )(*ops)


def solution(mesh):
    both = ("region", "wave")
    placed = (
        P(None, None, both), P(None, None, both), P(None, None, both), P(None, None, both), P(None, both),
        P(None, None, both), P(None, both), P(), P(), P(), P(None, both), P(None, both), P(None, both),
        P(both, None), P(both), P(both), P(None, both), P(None, both), P(both),
    )
    return jax.shard_map(
        body, mesh=mesh, in_specs=placed,
        out_specs=(P(None, None, both), P(None, None, both), P(None, both)), check_vma=False,
    )
```

profile of v0, /device:TPU:1, one launch (start us, length us, event | category | flops | bytes accessed | tf_op | source)
XLA Modules:
  0.0 48.5 jit_solution(14998787372079418187)
XLA Ops:
  0.6 0.0 copy-start.13
  0.7 0.0 copy-start.14
  0.7 0.0 copy-start.17
  0.7 0.7 %copy-done.13 = s32[16,128]{1,0:T(8,128)S(1)} copy-done((s32[16,128]{1,0:T(8,128)S(1)}, s32[16,128]{1,0:T(8,128)}, u32[]{:S(2)}) %copy-start.13) | copy-done | bytes 8216
  1.3 0.0 copy-done.14
  1.3 0.0 copy-done.17
  1.4 0.0 copy-start
  1.4 1.0 %copy-done = f32[9,35,256]{2,1,0:T(8,128)S(1)} copy-done((f32[9,35,256]{2,1,0:T(8,128)S(1)}, f32[9,35,256]{2,1,0:T(8,128)}, u32[]{:S(2)}) %copy-start) | copy-done | bytes 322584
  2.3 0.0 copy-start.1
  2.3 1.0 %copy-done.1 = f32[9,35,256]{2,1,0:T(8,128)S(1)} copy-done((f32[9,35,256]{2,1,0:T(8,128)S(1)}, f32[9,35,256]{2,1,0:T(8,128)}, u32[]{:S(2)}) %copy-start.1) | copy-done | bytes 322584
  3.3 0.0 copy-start.2
  3.3 1.0 %copy-done.2 = f32[9,35,256]{2,1,0:T(8,128)S(1)} copy-done((f32[9,35,256]{2,1,0:T(8,128)S(1)}, f32[9,35,256]{2,1,0:T(8,128)}, u32[]{:S(2)}) %copy-start.2) | copy-done | bytes 322584
  4.3 0.0 copy-start.3
  4.3 0.9 %copy-done.3 = f32[3,35,256]{2,1,0:T(8,128)S(1)} copy-done((f32[3,35,256]{2,1,0:T(8,128)S(1)}, f32[3,35,256]{2,1,0:T(8,128)}, u32[]{:S(2)}) %copy-start.3) | copy-done | bytes 107544
  5.2 0.0 copy-start.4
  5.2 0.8 %copy-done.4 = bf16[128,144]{1,0:T(8,128)(2,1)S(1)} copy-done((bf16[128,144]{1,0:T(8,128)(2,1)S(1)}, bf16[128,144]{1,0:T(8,128)(2,1)}, u32[]{:S(2)}) %copy-start.4) | copy-done | bytes 36888
  6.1 0.0 copy-start.5
  6.1 0.8 %copy-done.5 = f32[3,35,35]{2,1,0:T(8,128)S(1)} copy-done((f32[3,35,35]{2,1,0:T(8,128)S(1)}, f32[3,35,35]{2,1,0:T(8,128)}, u32[]{:S(2)}) %copy-start.5) | copy-done | bytes 14724
  6.9 0.0 copy-start.6
  6.9 0.8 %copy-done.6 = f32[8,35,10]{1,0,2:T(8,128)S(1)} copy-done((f32[8,35,10]{1,0,2:T(8,128)S(1)}, f32[8,35,10]{1,0,2:T(8,128)}, u32[]{:S(2)}) %copy-start.6) | copy-done | bytes 11224
  7.7 0.0 copy-start.7
  7.7 0.8 %copy-done.7 = f32[35,256]{1,0:T(8,128)S(1)} copy-done((f32[35,256]{1,0:T(8,128)S(1)}, f32[35,256]{1,0:T(8,128)}, u32[]{:S(2)}) %copy-start.7) | copy-done | bytes 35864
  8.4 0.0 copy-start.8
  8.4 0.8 %copy-done.8 = f32[4,35,15]{1,0,2:T(4,128)S(1)} copy-done((f32[4,35,15]{1,0,2:T(4,128)S(1)}, f32[4,35,15]{1,0,2:T(4,128)}, u32[]{:S(2)}) %copy-start.8) | copy-done | bytes 8424
  9.2 0.0 copy-start.9
  9.2 0.7 %copy-done.9 = f32[9,256]{1,0:T(8,128)S(1)} copy-done((f32[9,256]{1,0:T(8,128)S(1)}, f32[9,256]{1,0:T(8,128)}, u32[]{:S(2)}) %copy-start.9) | copy-done | bytes 9240
  9.9 0.0 copy-start.10
  9.9 0.7 %copy-done.10 = f32[30,32]{1,0:T(8,128)S(1)} copy-done((f32[30,32]{1,0:T(8,128)S(1)}, f32[30,32]{1,0:T(8,128)}, u32[]{:S(2)}) %copy-start.10) | copy-done | bytes 3864
  10.6 0.0 copy-start.11
  10.6 0.7 %copy-done.11 = f32[30,32]{1,0:T(8,128)S(1)} copy-done((f32[30,32]{1,0:T(8,128)S(1)}, f32[30,32]{1,0:T(8,128)}, u32[]{:S(2)}) %copy-start.11) | copy-done | bytes 3864
  11.4 0.0 copy-start.12
  11.4 0.7 %copy-done.12 = f32[3,4,256]{2,1,0:T(4,128)S(1)} copy-done((f32[3,4,256]{2,1,0:T(4,128)S(1)}, f32[3,4,256]{2,1,0:T(4,128)}, u32[]{:S(2)}) %copy-start.12) | copy-done | bytes 12312
  12.1 0.0 copy-start.15
  12.1 0.7 %copy-done.15 = s32[4,256]{1,0:T(4,128)S(1)} copy-done((s32[4,256]{1,0:T(4,128)S(1)}, s32[4,256]{1,0:T(4,128)}, u32[]{:S(2)}) %copy-start.15) | copy-done | bytes 4120
  12.7 0.0 copy-start.16
  12.8 0.7 %copy-done.16 = s32[4,256]{1,0:T(4,128)S(1)} copy-done((s32[4,256]{1,0:T(4,128)S(1)}, s32[4,256]{1,0:T(4,128)}, u32[]{:S(2)}) %copy-start.16) | copy-done | bytes 4120
  13.4 0.0 copy-start.18
  13.4 0.7 %copy-done.18 = s32[256]{0:T(256)S(1)} copy-done((s32[256]{0:T(256)S(1)}, s32[256]{0:T(256)}, u32[]{:S(2)}) %copy-start.18) | copy-done | bytes 1048
  14.1 0.0 copy-start.19
  14.1 0.7 %copy-done.19 = s32[256]{0:T(256)S(1)} copy-done((s32[256]{0:T(256)S(1)}, s32[256]{0:T(256)}, u32[]{:S(2)}) %copy-start.19) | copy-done | bytes 1048
  14.8 0.0 copy-start.20
  14.8 0.7 %copy-done.20 = s32[128]{0:T(128)S(1)} copy-done((s32[128]{0:T(128)S(1)}, s32[128]{0:T(128)}, u32[]{:S(2)}) %copy-start.20) | copy-done | bytes 536
  15.4 30.9 %shard_map.220 = (f32[9,35,256]{2,1,0:T(8,128)S(1)}, f32[9,35,256]{2,1,0:T(8,128)S(1)}, f32[30,32]{1,0:T(8,128)S(1)}) custom-call(f32[9,35,256]{2,1,0:T(8,128)S(1)} %copy-done, f32[9,35,256]{2,1,0:T(8,128)S(1)} %copy-done.1, f32[9,35,256]{2,1,0:T(8,128)S(1)} %copy-done.2, f32[3,35,256]{2,1,0:T(8,128)S(1)} %copy-done.3, f32[9,256]{1,0:T(8,128)S(1)} %copy-done.9, ...), custom_call_target="tpu_custom_call" | custom-call | tf_op jit(solution)/shard_map/pallas_call | solution.py:350
  46.4 0.7 %copy.27 = f32[9,35,256]{2,1,0:T(8,128)} copy(f32[9,35,256]{2,1,0:T(8,128)S(1)} %get-tuple-element.6) | data formatting | bytes 645120
  47.1 0.7 %copy.28 = f32[9,35,256]{2,1,0:T(8,128)} copy(f32[9,35,256]{2,1,0:T(8,128)S(1)} %get-tuple-element.7) | data formatting | bytes 645120
  47.9 0.6 %copy.29 = f32[30,32]{1,0:T(8,128)} copy(f32[30,32]{1,0:T(8,128)S(1)} %get-tuple-element.8) | data formatting | bytes 7680
Async XLA Ops:
  0.6 0.7 %copy-start.13 = (s32[16,128]{1,0:T(8,128)S(1)}, s32[16,128]{1,0:T(8,128)}, u32[]{:S(2)}) copy-start(s32[16,128]{1,0:T(8,128)} %constant.5.clone.turn) | copy-start | bytes 24580
  0.7 0.7 %copy-start.14 = (f32[4,256]{1,0:T(4,128)S(1)}, f32[4,256]{1,0:T(4,128)}, u32[]{:S(2)}) copy-start(f32[4,256]{1,0:T(4,128)} %face_scale.1) | copy-start | bytes 12292
  0.7 0.7 %copy-start.17 = (s32[256,1]{0,1:T(1,128)S(1)}, s32[256,1]{0,1:T(1,128)}, u32[]{:S(2)}) copy-start(s32[256,1]{0,1:T(1,128)} %param.34) | copy-start | bytes 3076
  1.4 1.0 %copy-start = (f32[9,35,256]{2,1,0:T(8,128)S(1)}, f32[9,35,256]{2,1,0:T(8,128)}, u32[]{:S(2)}) copy-start(f32[9,35,256]{2,1,0:T(8,128)} %s0.1) | copy-start | bytes 967684
  2.3 1.0 %copy-start.1 = (f32[9,35,256]{2,1,0:T(8,128)S(1)}, f32[9,35,256]{2,1,0:T(8,128)}, u32[]{:S(2)}) copy-start(f32[9,35,256]{2,1,0:T(8,128)} %dl.1) | copy-start | bytes 967684
  3.3 1.0 %copy-start.2 = (f32[9,35,256]{2,1,0:T(8,128)S(1)}, f32[9,35,256]{2,1,0:T(8,128)}, u32[]{:S(2)}) copy-start(f32[9,35,256]{2,1,0:T(8,128)} %ad.1) | copy-start | bytes 967684
  4.3 0.9 %copy-start.3 = (f32[3,35,256]{2,1,0:T(8,128)S(1)}, f32[3,35,256]{2,1,0:T(8,128)}, u32[]{:S(2)}) copy-start(f32[3,35,256]{2,1,0:T(8,128)} %model.1) | copy-start | bytes 322564
  5.2 0.8 %copy-start.4 = (bf16[128,144]{1,0:T(8,128)(2,1)S(1)}, bf16[128,144]{1,0:T(8,128)(2,1)}, u32[]{:S(2)}) copy-start(bf16[128,144]{1,0:T(8,128)(2,1)} %constant.4.clone.pick) | copy-start | bytes 110596
  6.1 0.8 %copy-start.5 = (f32[3,35,35]{2,1,0:T(8,128)S(1)}, f32[3,35,35]{2,1,0:T(8,128)}, u32[]{:S(2)}) copy-start(f32[3,35,35]{2,1,0:T(8,128)} %derivative.1) | copy-start | bytes 44104
  6.9 0.8 %copy-start.6 = (f32[8,35,10]{1,0,2:T(8,128)S(1)}, f32[8,35,10]{1,0,2:T(8,128)}, u32[]{:S(2)}) copy-start(f32[8,35,10]{1,0,2:T(8,128)} %param.30) | copy-start | bytes 33604
  7.7 0.8 %copy-start.7 = (f32[35,256]{1,0:T(8,128)S(1)}, f32[35,256]{1,0:T(8,128)}, u32[]{:S(2)}) copy-start(f32[35,256]{1,0:T(8,128)} %observe.1) | copy-start | bytes 107524
  8.4 0.8 %copy-start.8 = (f32[4,35,15]{1,0,2:T(4,128)S(1)}, f32[4,35,15]{1,0,2:T(4,128)}, u32[]{:S(2)}) copy-start(f32[4,35,15]{1,0,2:T(4,128)} %param.29) | copy-start | bytes 25204
  9.2 0.7 %copy-start.9 = (f32[9,256]{1,0:T(8,128)S(1)}, f32[9,256]{1,0:T(8,128)}, u32[]{:S(2)}) copy-start(f32[9,256]{1,0:T(8,128)} %geometry.1) | copy-start | bytes 27652
  9.9 0.7 %copy-start.10 = (f32[30,32]{1,0:T(8,128)S(1)}, f32[30,32]{1,0:T(8,128)}, u32[]{:S(2)}) copy-start(f32[30,32]{1,0:T(8,128)} %coarse.1) | copy-start | bytes 11524
  10.6 0.7 %copy-start.11 = (f32[30,32]{1,0:T(8,128)S(1)}, f32[30,32]{1,0:T(8,128)}, u32[]{:S(2)}) copy-start(f32[30,32]{1,0:T(8,128)} %reg.1) | copy-start | bytes 11524
  11.4 0.7 %copy-start.12 = (f32[3,4,256]{2,1,0:T(4,128)S(1)}, f32[3,4,256]{2,1,0:T(4,128)}, u32[]{:S(2)}) copy-start(f32[3,4,256]{2,1,0:T(4,128)} %normals.1) | copy-start | bytes 36868
  12.1 0.7 %copy-start.15 = (s32[4,256]{1,0:T(4,128)S(1)}, s32[4,256]{1,0:T(4,128)}, u32[]{:S(2)}) copy-start(s32[4,256]{1,0:T(4,128)} %neighbor.1) | copy-start | bytes 12292
  12.7 0.7 %copy-start.16 = (s32[4,256]{1,0:T(4,128)S(1)}, s32[4,256]{1,0:T(4,128)}, u32[]{:S(2)}) copy-start(s32[4,256]{1,0:T(4,128)} %orient.1) | copy-start | bytes 12292
  13.4 0.7 %copy-start.18 = (s32[256]{0:T(256)S(1)}, s32[256]{0:T(256)}, u32[]{:S(2)}) copy-start(s32[256]{0:T(256)} %param.35) | copy-start | bytes 3076
  14.1 0.7 %copy-start.19 = (s32[256]{0:T(256)S(1)}, s32[256]{0:T(256)}, u32[]{:S(2)}) copy-start(s32[256]{0:T(256)} %param.36) | copy-start | bytes 3076
  14.8 0.7 %copy-start.20 = (s32[128]{0:T(128)S(1)}, s32[128]{0:T(128)}, u32[]{:S(2)}) copy-start(s32[128]{0:T(128)} %param.39) | copy-start | bytes 1540
where the time goes:
time: 49.4 us; the launch traced here: 48.5 us
  Pallas kernels  30.9 us (63%)
  local copies, waits for them, and re-layouts  16.9 us (34%)
  between operations  0.69 us (1%)
    pallas_call x1, Pallas kernels, body(): pl.pallas_call(kernel, out_shape=(jax.ShapeDtypeStruct((NF, NN, E), f32),...  30.9 us
    unnamed x45, local copies, waits for them, and re-layouts  16.9 us

commit v1 on v0

--- a/solution.py
+++ b/solution.py
@@ -86,7 +86,21 @@
     return jnp.concatenate([hi, lo, hi], axis=0)
 
 
-def kernel(
+N_OPS = 21
+
+
+def kernel(*refs):
+    sources, (out_d, out_a, out_h) = refs[:N_OPS], refs[N_OPS:N_OPS + 3]
+    held = refs[N_OPS + 3:2 * N_OPS + 3]
+    isem = refs[-1]
+    loads = [pltpu.make_async_copy(a, b, isem.at[at]) for at, (a, b) in enumerate(zip(sources, held))]
+    for load in loads:
+        load.start()
+    work(loads, *held, out_d, out_a, out_h, *refs[2 * N_OPS + 3:-1])
+
+
+def work(
+    loads,
     s0, dl, ad, model, geometry, normals, face_scale, derivative, lift, prolong, coarse, reg, observe,
     owner, local, child, neighbor, orient, send_face, pick, turn,
     out_d, out_a, out_h,
@@ -123,6 +137,9 @@
     def wait_rows(ref, sem):
         part = ref.at[pl.ds(0, ND - 1)]
         pltpu.make_async_copy(part, part, sem).wait()
+
+    for load in loads:
+        load.wait()
 
     u = (iota((ND, E), 0) == owner[...]).astype(f32).astype(bf16)
     ub = u.astype(f32)
@@ -334,6 +351,15 @@
     wait_rows(pt_s, ssem.at[3])
 
 
+def place(*refs):
+    sem = refs[-1]
+    copies = [pltpu.make_async_copy(refs[at], refs[3 + at], sem.at[at]) for at in range(3)]
+    for copy in copies:
+        copy.start()
+    for copy in copies:
+        copy.wait()
+
+
 def body(
     state0, delta, adjoint, model, geometry, normals, face_scale, derivative, lift, prolong, coarse_step, reg_weight,
     observe, owner, coarse_local, child, neighbor, orient, send_face,
@@ -346,17 +372,21 @@
         jnp.asarray(pick, bf16), jnp.asarray(turn),
     )
     vmem = pl.BlockSpec(memory_space=pltpu.VMEM)
+    anywhere = pl.BlockSpec(memory_space=pl.ANY)
+    hbm = pl.BlockSpec(memory_space=pltpu.HBM)
     row = pltpu.VMEM((ND, 1, 128), f32)
-    return pl.pallas_call(
+    results = (
+        jax.ShapeDtypeStruct((NF, NN, E), f32),
+        jax.ShapeDtypeStruct((NF, NN, E), f32),
+        jax.ShapeDtypeStruct((30, 32), f32),
+    )
+    found = pl.pallas_call(
         kernel,
-        out_shape=(
-            jax.ShapeDtypeStruct((NF, NN, E), f32),
-            jax.ShapeDtypeStruct((NF, NN, E), f32),
-            jax.ShapeDtypeStruct((30, 32), f32),
-        ),
-        in_specs=[vmem] * len(ops),
+        out_shape=results,
+        in_specs=[hbm] * len(ops),
         out_specs=(vmem, vmem, vmem),
         scratch_shapes=[
+            *(pltpu.VMEM(op.shape, op.dtype) for op in ops),
             pltpu.VMEM((2, ROWS, TAB), bf16),
             pltpu.VMEM((TAB, OWN), bf16),
             pltpu.VMEM((27, 120, E), f32),
@@ -372,11 +402,20 @@
             row, row, row, row, row, row,
             pltpu.SemaphoreType.DMA((4,)),
             pltpu.SemaphoreType.DMA((4,)),
+            pltpu.SemaphoreType.DMA((N_OPS,)),
         ],
         compiler_params=pltpu.CompilerParams(
-            collective_id=0, has_side_effects=True, vmem_limit_bytes=48 * 1024 * 1024
+            collective_id=0, has_side_effects=True, vmem_limit_bytes=60 * 1024 * 1024
         ),
     )(*ops)
+    return pl.pallas_call(
+        place,
+        out_shape=results,
+        in_specs=[anywhere] * 3,
+        out_specs=(hbm, hbm, hbm),
+        scratch_shapes=[pltpu.SemaphoreType.DMA((3,))],
+        compiler_params=pltpu.CompilerParams(vmem_limit_bytes=60 * 1024 * 1024),
+    )(*found)
 
 
 def solution(mesh):

time: 49.4 us -> 56.9 us (1.15); the launches traced: 48.5 us -> 56.8 us
  Pallas kernels: 30.9 us -> 56.1 us
  local copies, waits for them, and re-layouts: 16.9 us -> 0 us
    pallas_call x1 -> x2, Pallas kernels: 30.9 us -> 56.1 us  [the longest x1 32.2 us: body(): pl.pallas_call(kernel, out_shape=results, in_specs=[hbm] * len(ops), out_...]
    unnamed x45 -> x0, local copies, waits for them, and re-layouts: 16.9 us -> none
where the time goes in v1:
time: 56.9 us; the launch traced here: 56.8 us
  Pallas kernels  56.1 us (99%)
  between operations  0.65 us (1%)
    pallas_call x1, Pallas kernels, body(): pl.pallas_call(kernel, out_shape=results, in_specs=[hbm] * len(ops), out_...  32.2 us
    pallas_call x1, Pallas kernels, body(): pl.pallas_call(place, out_shape=results, in_specs=[anywhere] * 3, out_spe...  23.9 us

profile of v1, /device:TPU:1, one launch (start us, length us, event | category | flops | bytes accessed | tf_op | source)
XLA Modules:
  0.0 56.8 jit_solution(16996467279205300374)
XLA Ops:
  0.6 32.2 %shard_map.220 = (f32[9,35,256]{2,1,0:T(8,128)}, f32[9,35,256]{2,1,0:T(8,128)}, f32[30,32]{1,0:T(8,128)}) custom-call(f32[9,35,256]{2,1,0:T(8,128)} %refs_0_.1, f32[9,35,256]{2,1,0:T(8,128)} %refs_1_.1, f32[9,35,256]{2,1,0:T(8,128)} %refs_2_.1, f32[3,35,256]{2,1,0:T(8,128)} %refs_3_.1, f32[9,256]{1,0:T(8,128)} %refs_4_.1, f32[3,4,256]{2,1,0:T(4,128)} %refs_5_.1, ...), custom_call_target="tpu_custom_call" | custom-call | tf_op jit(solution)/shard_map/pallas_call | solution.py:383
  32.8 23.9 %shard_map.221 = (f32[9,35,256]{2,1,0:T(8,128)}, f32[9,35,256]{2,1,0:T(8,128)}, f32[30,32]{1,0:T(8,128)}) custom-call(f32[9,35,256]{2,1,0:T(8,128)} %get-tuple-element.6.refs_0_, f32[9,35,256]{2,1,0:T(8,128)} %get-tuple-element.7.refs_1_, f32[30,32]{1,0:T(8,128)} %get-tuple-element.8.refs_2_), custom_call_target="tpu_custom_call" | custom-call | tf_op jit(solution)/shard_map/pallas_call | solution.py:411

commit v2 on v1

--- a/solution.py
+++ b/solution.py
@@ -105,49 +105,53 @@
     owner, local, child, neighbor, orient, send_face, pick, turn,
     out_d, out_a, out_h,
     tab, hot, dq, jump, hn, xl, fs, ltr, rst, c1,
-    tr_s, tr_r, rq_s, rq_r, an_s, an_r, pt_s, pt_r,
-    ssem, rsem,
+    tr_s, tr_r, ag_s, ag_r, p1, p2, p3, chot, new_d, new_a,
+    ssem, rsem, osem,
 ):
     region, wave = lax.axis_index("region"), lax.axis_index("wave")
     me = region * NW + wave
+    core = lax.rem(wave, 2)
+    chip = lax.div(me, 2)
     barrier = pltpu.get_barrier_semaphore()
 
-    def where_is(i):
-        d = lax.rem(me + i, ND)
-        return d, (lax.div(d, NW), lax.rem(d, NW))
-
-    def greet(i, c):
-        pl.semaphore_signal(barrier, inc=1, device_id=where_is(i)[1], device_id_type=MESH)
-        return c
-
-    lax.fori_loop(1, ND, greet, 0)
-
-    def send_rows(src, dst, at):
+    def greet(there):
+        pl.semaphore_signal(barrier, inc=1, device_id=there, device_id_type=MESH)
+
+    def alike(i):
+        d = lax.rem(me + 2 * i, ND)
+        return lax.div(d, 2), (lax.div(d, NW), lax.rem(d, NW))
+
+    def each(low, high, act):
         def one(i, c):
-            d, there = where_is(i)
-            pltpu.make_async_remote_copy(
-                src_ref=src.at[d], dst_ref=dst.at[me], send_sem=ssem.at[at], recv_sem=rsem.at[at],
-                device_id=there, device_id_type=MESH,
-            ).start()
+            act(i)
             return c
 
-        lax.fori_loop(1, ND, one, 0)
-        dst[pl.ds(me, 1)] = src[pl.ds(me, 1)]
-
-    def wait_rows(ref, sem):
-        part = ref.at[pl.ds(0, ND - 1)]
+        lax.fori_loop(low, high, one, 0)
+
+    sibling = (region, wave + 1 - 2 * core)
+    each(0, 16, lambda i: greet((region, lax.rem(wave + 2 * i + 1, NW))))
+    each(1, 64, lambda i: greet(alike(i)[1]))
+
+    def send(src, dst, at, there):
+        pltpu.make_async_remote_copy(
+            src_ref=src, dst_ref=dst, send_sem=ssem.at[at], recv_sem=rsem.at[at], device_id=there, device_id_type=MESH
+        ).start()
+
+    def wait(part, sem):
         pltpu.make_async_copy(part, part, sem).wait()
 
     for load in loads:
         load.wait()
+
+    cs = jnp.concatenate([coarse[...], jnp.zeros((2, 32), f32)], axis=0)
+    cst = jnp.concatenate([cs, jnp.zeros((32, 96), f32)], axis=1).T
+    ag_s[...] = jnp.concatenate([cst[q * 8:q * 8 + 8, 0:32] for q in range(4)], axis=1)
+    ag_r[pl.ds(chip, 1), pl.ds(core, 1)] = ag_s[...].reshape(1, 1, 8, 128)
 
     u = (iota((ND, E), 0) == owner[...]).astype(f32).astype(bf16)
     ub = u.astype(f32)
     tri = (iota((E, E), 0) < iota((E, E), 1)).astype(f32).astype(bf16)
     before = jnp.sum(nn(u, tri) * ub, axis=0, keepdims=True).astype(i32)
-    code = before * 32 + local[...]
-    vt = (iota((128, E), 0) == code).astype(f32).astype(bf16)
-    rq_s.reshape(ND, 128)[...] = nt(u, vt)
 
     for k in range(3):
         c1[k * 40:(k + 1) * 40, :] = lanes3(below(derivative[k], 40), 48)
@@ -168,18 +172,14 @@
     for j in range(4):
         tr_s.reshape(4, 128, 128)[j] = sent[j * 128:(j + 1) * 128].T
 
-    pl.semaphore_wait(barrier, ND - 1)
-    send_rows(rq_s, rq_r, 0)
-
-    def send_trace(i, c):
+    pl.semaphore_wait(barrier, 79)
+
+    def send_trace(i):
         w = lax.rem(wave + i, NW)
-        pltpu.make_async_remote_copy(
-            src_ref=tr_s.at[:, pl.ds(w, 1)], dst_ref=tr_r.at[:, pl.ds(wave, 1)],
-            send_sem=ssem.at[1], recv_sem=rsem.at[1], device_id=(region, w), device_id_type=MESH,
-        ).start()
-        return c
-
-    lax.fori_loop(1, NW, send_trace, 0)
+        send(tr_s.at[:, pl.ds(w, 1)], tr_r.at[:, pl.ds(wave, 1)], 0, (region, w))
+
+    each(1, NW, send_trace)
+    each(1, 64, lambda i: send(ag_s, ag_r.at[chip, core], 1, alike(i)[1]))
     tr_r[:, pl.ds(wave, 1)] = tr_s[:, pl.ds(wave, 1)]
 
     for f in range(4):
@@ -188,22 +188,17 @@
             iota((TAB, E), 0, i16) == row, jnp.ones((), bf16), jnp.zeros((), bf16)
         )
 
-    wait_rows(rq_r, rsem.at[0])
-    asked = rq_r.reshape(ND, 128)[...].astype(bf16)
-    cs = jnp.concatenate([coarse[...], jnp.zeros((2, 32), f32)], axis=0)
-    cs4 = jnp.concatenate([cs] * 4, axis=1)
-    cs16 = jnp.concatenate([cs4] * 4, axis=0)
-    same = lax.div(iota((128, 128), 0), 32) == lax.div(iota((128, 128), 1), 32)
-    bh, bl = split(jnp.where(same, cs16, 0.0))
-    an_s.reshape(ND, 128)[...] = nt(asked, bh) + nt(asked, bl)
-    send_rows(an_s, an_r, 2)
+    line = (owner[...] * 8 + (local[...] & 7)).astype(i16)
+    chot[...] = jnp.where(iota((1024, E), 0, i16) == line, jnp.ones((), bf16), jnp.zeros((), bf16))
 
     for f in range(4):
         span = slice(f * E, (f + 1) * E)
         jump[:, span] = nn(tab[0, :, 0:OWN], hot[0:OWN, span]) + nn(tab[1, :, 0:OWN], hot[0:OWN, span])
 
-    part = tr_r.at[:, pl.ds(0, NW - 1)]
-    pltpu.make_async_copy(part, part, rsem.at[1]).wait()
+    wait(ag_r.at[pl.ds(0, 63), 0], rsem.at[1])
+    send(ag_r.at[:, pl.ds(core, 1)], ag_r.at[:, pl.ds(core, 1)], 2, sibling)
+
+    wait(tr_r.at[:, pl.ds(0, NW - 1)], rsem.at[0])
     for j in range(4):
         rows = min(128, ROWS - j * 128)
         hi, lo = split(tr_r.reshape(4, 128, 128)[j].T[0:rows])
@@ -277,10 +272,11 @@
             for c in range(NF):
                 fs[s, 9 + c] = nn(lmat, xl[9 + c])
 
-    wait_rows(an_r, rsem.at[2])
-    ah, al = split(an_r.reshape(ND, 128)[...])
-    slot = lax.div(iota((128, E), 0), 32) == before
-    found = jnp.where(slot, tn(ah, u) + tn(al, u), 0.0)
+    wait(ag_r.at[:, pl.ds(0, 1)], rsem.at[2])
+    chi, clo = split(ag_r[...].reshape(1024, 128).T)
+    found = jnp.where(
+        lax.div(iota((128, E), 0), 32) == lax.shift_right_logical(local[...], 3), nn(chi, chot[...]) + nn(clo, chot[...]), 0.0
+    )
     found = found[0:32] + found[32:64] + found[64:96] + found[96:128]
     mask = (iota((8, E), 0) == child[...]).astype(f32)
     pm = prolong[...].reshape(80, NN)
@@ -319,45 +315,69 @@
                 wave_a = wave_a + lam2
         nd = below(dl[c], 40) + STEP * (wave_d + fs[1, 9 + c])
         na = below(ad[c], 40) + STEP * (wave_a + fs[2, 9 + c] + obs * nd)
-        out_d[c] = nd[0:NN]
-        out_a[c] = na[0:NN]
+        new_d[c] = nd[0:NN]
+        new_a[c] = na[0:NN]
         if c < 3:
             gb = gb + na * fs[0, c]
         else:
             gm = gm + na * mu(0, c - 3)
             if c < 6:
                 tr = tr + na
+    stores = [pltpu.make_async_copy(new_d, out_d, osem.at[0]), pltpu.make_async_copy(new_a, out_a, osem.at[1])]
+    for store in stores:
+        store.start()
     fine_grad = (STEP * gb, STEP * tr * lam0, STEP * gm)
 
     pm144 = lanes3(pm, 48)
-    rst[...] = jnp.zeros_like(rst)
+    rst[30:31, :] = local[...].astype(f32)
+    rst[31:32, :] = jnp.zeros((1, E), f32)
     for p in range(3):
         r = nn(pm144, rows3(below(fine_grad[p], 48)))
         rst[p * 10:(p + 1) * 10, :] = jnp.sum(r.reshape(10, 8, E) * mask[None], axis=1)
+    slot = lax.div(iota((128, E), 0), 32) == before
     wh, wl = split(jnp.where(slot, jnp.concatenate([rst[...]] * 4, axis=0), 0.0))
-    pt_s.reshape(ND, 128)[...] = nt(u, wh) + nt(u, wl)
-    send_rows(pt_s, pt_r, 3)
-    wait_rows(pt_r, rsem.at[3])
-    gh, gl = split(pt_r.reshape(ND, 128)[...])
+    p1.reshape(ND, 128)[...] = nt(u, wh) + nt(u, wl)
+    send(p1.at[:, pl.ds(1 - core, 1)], p2.at[:, pl.ds(core, 1)], 3, sibling)
+    p2[:, pl.ds(core, 1)] = p1[:, pl.ds(core, 1)]
+    wait(p2.at[:, pl.ds(0, 1)], rsem.at[3])
+
+    def send_partial(i):
+        to, there = alike(i)
+        send(p2.at[to], p3.at[chip], 4, there)
+
+    each(1, 64, send_partial)
+    p3[pl.ds(chip, 1)] = p2[pl.ds(chip, 1)]
+    wait(p3.at[pl.ds(0, 63)], rsem.at[4])
+    gh, gl = split(p3.reshape(ND, 128)[...])
+    place_of = lax.rem(iota((128, 128), 1), 32)
+    spread = (iota((128, 128), 0) == iota((128, 128), 1) - place_of + 30).astype(f32).astype(bf16)
+    asked = (nn(gh, spread).astype(i32) == place_of).astype(f32).astype(bf16)
+    same = lax.div(iota((128, 128), 0), 32) == lax.div(iota((128, 128), 1), 32)
     total = jnp.where(same, tn(gh, asked) + tn(gl, asked), 0.0)
     total = total[0:32] + total[32:64] + total[64:96] + total[96:128]
     total = total[:, 0:32] + total[:, 32:64] + total[:, 64:96] + total[:, 96:128]
     out_h[...] = total[0:30] + reg[...] * coarse[...]
 
-    wait_rows(rq_s, ssem.at[0])
-    part = tr_s.at[:, pl.ds(0, NW - 1)]
-    pltpu.make_async_copy(part, part, ssem.at[1]).wait()
-    wait_rows(an_s, ssem.at[2])
-    wait_rows(pt_s, ssem.at[3])
+    wait(tr_s.at[:, pl.ds(0, NW - 1)], ssem.at[0])
+    wait(ag_r.at[pl.ds(0, 63), 0], ssem.at[1])
+    wait(ag_r.at[:, pl.ds(0, 1)], ssem.at[2])
+    wait(p1.at[:, pl.ds(0, 1)], ssem.at[3])
+    wait(p2.at[pl.ds(0, 63)], ssem.at[4])
+    for store in stores:
+        store.wait()
 
 
 def place(*refs):
-    sem = refs[-1]
-    copies = [pltpu.make_async_copy(refs[at], refs[3 + at], sem.at[at]) for at in range(3)]
-    for copy in copies:
-        copy.start()
-    for copy in copies:
-        copy.wait()
+    isem, osem = refs[-2:]
+    loads = [pltpu.make_async_copy(refs[at], refs[6 + at], isem.at[at]) for at in range(3)]
+    stores = [pltpu.make_async_copy(refs[6 + at], refs[3 + at], osem.at[at]) for at in range(3)]
+    for load in loads:
+        load.start()
+    for load, store in zip(loads, stores):
+        load.wait()
+        store.start()
+    for store in stores:
+        store.wait()
 
 
 def body(
@@ -374,7 +394,7 @@
     vmem = pl.BlockSpec(memory_space=pltpu.VMEM)
     anywhere = pl.BlockSpec(memory_space=pl.ANY)
     hbm = pl.BlockSpec(memory_space=pltpu.HBM)
-    row = pltpu.VMEM((ND, 1, 128), f32)
+    row = pltpu.VMEM((64, 2, 1, 128), f32)
     results = (
         jax.ShapeDtypeStruct((NF, NN, E), f32),
         jax.ShapeDtypeStruct((NF, NN, E), f32),
@@ -384,7 +404,7 @@
         kernel,
         out_shape=results,
         in_specs=[hbm] * len(ops),
-        out_specs=(vmem, vmem, vmem),
+        out_specs=(hbm, hbm, vmem),
         scratch_shapes=[
             *(pltpu.VMEM(op.shape, op.dtype) for op in ops),
             pltpu.VMEM((2, ROWS, TAB), bf16),
@@ -399,9 +419,15 @@
             pltpu.VMEM((248, 144), bf16),
             pltpu.VMEM((4, NW, 4, 128), f32),
             pltpu.VMEM((4, NW, 4, 128), f32),
-            row, row, row, row, row, row,
-            pltpu.SemaphoreType.DMA((4,)),
-            pltpu.SemaphoreType.DMA((4,)),
+            pltpu.VMEM((8, 128), f32),
+            pltpu.VMEM((64, 2, 8, 128), f32),
+            row, row, row,
+            pltpu.VMEM((1024, E), bf16),
+            pltpu.VMEM((NF, NN, E), f32),
+            pltpu.VMEM((NF, NN, E), f32),
+            pltpu.SemaphoreType.DMA((5,)),
+            pltpu.SemaphoreType.DMA((5,)),
+            pltpu.SemaphoreType.DMA((2,)),
             pltpu.SemaphoreType.DMA((N_OPS,)),
         ],
         compiler_params=pltpu.CompilerParams(
@@ -413,7 +439,11 @@
         out_shape=results,
         in_specs=[anywhere] * 3,
         out_specs=(hbm, hbm, hbm),
-        scratch_shapes=[pltpu.SemaphoreType.DMA((3,))],
+        scratch_shapes=[
+            *(pltpu.VMEM(r.shape, r.dtype) for r in results),
+            pltpu.SemaphoreType.DMA((3,)),
+            pltpu.SemaphoreType.DMA((3,)),
+        ],
         compiler_params=pltpu.CompilerParams(vmem_limit_bytes=60 * 1024 * 1024),
     )(*found)
 

time: 56.9 us -> 33.2 us (0.58)
  Pallas kernels: 56.1 us -> 32.4 us
    pallas_call x1, Pallas kernels: 23.9 us -> 1.9 us  [body(): pl.pallas_call(place, out_shape=results, in_specs=[anywhere] * 3, out_spe...]
    pallas_call x1, Pallas kernels: 32.2 us -> 30.5 us  [body(): pl.pallas_call(kernel, out_shape=results, in_specs=[hbm] * len(ops), out_...]
where the time goes in v2:
time: 33.2 us; the launch traced here: 33 us
  Pallas kernels  32.4 us (98%)
  between operations  0.65 us (2%)
    pallas_call x1, Pallas kernels, body(): pl.pallas_call(kernel, out_shape=results, in_specs=[hbm] * len(ops), out_...  30.5 us
    pallas_call x1, Pallas kernels, body(): pl.pallas_call(place, out_shape=results, in_specs=[anywhere] * 3, out_spe...  1.9 us

profile of v2, /device:TPU:1, one launch (start us, length us, event | category | flops | bytes accessed | tf_op | source)
XLA Modules:
  0.0 33.0 jit_solution(17416250799087579105)
XLA Ops:
  0.6 30.5 %shard_map.220 = (f32[9,35,256]{2,1,0:T(8,128)}, f32[9,35,256]{2,1,0:T(8,128)}, f32[30,32]{1,0:T(8,128)}) custom-call(f32[9,35,256]{2,1,0:T(8,128)} %refs_0_.1, f32[9,35,256]{2,1,0:T(8,128)} %refs_1_.1, f32[9,35,256]{2,1,0:T(8,128)} %refs_2_.1, f32[3,35,256]{2,1,0:T(8,128)} %refs_3_.1, f32[9,256]{1,0:T(8,128)} %refs_4_.1, f32[3,4,256]{2,1,0:T(4,128)} %refs_5_.1, ...), custom_call_target="tpu_custom_call" | custom-call | tf_op jit(solution)/shard_map/pallas_call | solution.py:403
  31.1 1.9 %shard_map.221 = (f32[9,35,256]{2,1,0:T(8,128)}, f32[9,35,256]{2,1,0:T(8,128)}, f32[30,32]{1,0:T(8,128)}) custom-call(f32[9,35,256]{2,1,0:T(8,128)} %get-tuple-element.6.refs_0_, f32[9,35,256]{2,1,0:T(8,128)} %get-tuple-element.7.refs_1_, f32[30,32]{1,0:T(8,128)} %get-tuple-element.8.refs_2_), custom_call_target="tpu_custom_call" | custom-call | tf_op jit(solution)/shard_map/pallas_call | solution.py:437

commit v3 on v2

--- a/solution.py
+++ b/solution.py
@@ -105,7 +105,7 @@
     owner, local, child, neighbor, orient, send_face, pick, turn,
     out_d, out_a, out_h,
     tab, hot, dq, jump, hn, xl, fs, ltr, rst, c1,
-    tr_s, tr_r, ag_s, ag_r, p1, p2, p3, chot, new_d, new_a,
+    tr_s, tr_r, ag_s, ag_r, p1, p2, p3, chot, new_d, new_a, lmat, order,
     ssem, rsem, osem,
 ):
     region, wave = lax.axis_index("region"), lax.axis_index("wave")
@@ -195,8 +195,46 @@
         span = slice(f * E, (f + 1) * E)
         jump[:, span] = nn(tab[0, :, 0:OWN], hot[0:OWN, span]) + nn(tab[1, :, 0:OWN], hot[0:OWN, span])
 
-    wait(ag_r.at[pl.ds(0, 63), 0], rsem.at[1])
-    send(ag_r.at[:, pl.ds(core, 1)], ag_r.at[:, pl.ds(core, 1)], 2, sibling)
+    for f in range(4):
+        span = slice(f * E, (f + 1) * E)
+        h = 0.5 * face_scale[f:f + 1, :]
+        for j in range(3):
+            hn[j, :, span] = jnp.broadcast_to(h * normals[j, f:f + 1, :], (8, E))
+        hn[3, :, span] = jnp.broadcast_to(h, (8, E))
+
+    ltr[...] = jnp.zeros_like(ltr)
+    for f in range(4):
+        for m in range(15):
+            ltr[f * 16 + m:f * 16 + m + 1, 0:NN] = lift[m, f:f + 1, :]
+    lh, ll = split(ltr[...].T[0:40])
+    lmat[...] = jnp.concatenate([lh.astype(f32), lh.astype(f32), ll.astype(f32)], axis=1).astype(bf16)
+
+    for f in range(4):
+        span = slice(f * E, (f + 1) * E)
+        idx = jnp.full((16, E), 15, i32)
+        for q in range(6):
+            idx = jnp.where(orient[f:f + 1, :] == q, turn[:, q:q + 1], idx)
+        order[:, span] = idx
+
+    geo = [geometry[q:q + 1, :] for q in range(9)]
+
+    def grad(sc, i):
+        return sum(geo[3 * i + k] * dq[sc, k * 40:(k + 1) * 40, :] for k in range(3))
+
+    for s in range(3):
+        base = s * NF
+        for i in range(3):
+            fs[s, i] = sum(grad(base + 3 + STRESS[i][j], j) for j in range(3))
+            fs[s, 3 + i] = grad(base + i, i)
+        for at, (i, j) in enumerate(OFF):
+            fs[s, 6 + at] = grad(base + j, i) + grad(base + i, j)
+
+    mask = (iota((8, E), 0) == child[...]).astype(f32)
+    pm = prolong[...].reshape(80, NN)
+    pm40 = jnp.concatenate([pm, jnp.zeros((80, 5), f32)], axis=1)
+    ph, pw = split(pm40)
+    pm3 = jnp.concatenate([ph, ph, pw], axis=0)
+    pm144 = lanes3(pm, 48)
 
     wait(tr_r.at[:, pl.ds(0, NW - 1)], rsem.at[0])
     for j in range(4):
@@ -210,24 +248,7 @@
 
     for f in range(4):
         span = slice(f * E, (f + 1) * E)
-        h = 0.5 * face_scale[f:f + 1, :]
-        for j in range(3):
-            hn[j, :, span] = jnp.broadcast_to(h * normals[j, f:f + 1, :], (8, E))
-        hn[3, :, span] = jnp.broadcast_to(h, (8, E))
-
-    ltr[...] = jnp.zeros_like(ltr)
-    for f in range(4):
-        for m in range(15):
-            ltr[f * 16 + m:f * 16 + m + 1, 0:NN] = lift[m, f:f + 1, :]
-    lh, ll = split(ltr[...].T[0:40])
-    lmat = jnp.concatenate([lh.astype(f32), lh.astype(f32), ll.astype(f32)], axis=1).astype(bf16)
-
-    for f in range(4):
-        span = slice(f * E, (f + 1) * E)
-        o = orient[f:f + 1, :]
-        idx = jnp.full((16, E), 15, i32)
-        for q in range(6):
-            idx = jnp.where(o == q, turn[:, q:q + 1], idx)
+        idx = order[:, span]
         low = idx < 8
         idx = idx & 7
         ia, ib = idx[0:8], idx[8:16]
@@ -242,12 +263,7 @@
                     jnp.where(low[t * 8:t * 8 + 8], ga, gb) - own[t * 8:t * 8 + 8]
                 )
 
-    geo = [geometry[q:q + 1, :] for q in range(9)]
-
-    def grad(sc, i):
-        return sum(geo[3 * i + k] * dq[sc, k * 40:(k + 1) * 40, :] for k in range(3))
-
-    for s in range(3):
+    def terms(s):
         for f in range(4):
             span = slice(f * E, (f + 1) * E)
             n = [jnp.concatenate([hn[j, :, span]] * 2, axis=0) for j in range(4)]
@@ -262,15 +278,19 @@
                 xl[at, f * 16:f * 16 + 16, :] = hi
                 xl[at, 64 + f * 16:80 + f * 16, :] = lo
                 xl[at, 128 + f * 16:144 + f * 16, :] = hi
-        base = s * NF
-        for i in range(3):
-            fs[s, i] = nn(lmat, xl[i]) + sum(grad(base + 3 + STRESS[i][j], j) for j in range(3))
-            fs[s, 3 + i] = nn(lmat, xl[3 + i]) + grad(base + i, i)
-        for at, (i, j) in enumerate(OFF):
-            fs[s, 6 + at] = nn(lmat, xl[6 + at]) + grad(base + j, i) + grad(base + i, j)
+        for at in range(9):
+            fs[s, at] += nn(lmat[...], xl[at])
         if s > 0:
-            for c in range(NF):
-                fs[s, 9 + c] = nn(lmat, xl[9 + c])
+            for at in range(9, 18):
+                fs[s, at] = nn(lmat[...], xl[at])
+
+    terms(0)
+
+    wait(ag_r.at[pl.ds(0, 63), 0], rsem.at[1])
+    send(ag_r.at[:, pl.ds(core, 1)], ag_r.at[:, pl.ds(core, 1)], 2, sibling)
+
+    terms(1)
+    terms(2)
 
     wait(ag_r.at[:, pl.ds(0, 1)], rsem.at[2])
     chi, clo = split(ag_r[...].reshape(1024, 128).T)
@@ -278,11 +298,6 @@
         lax.div(iota((128, E), 0), 32) == lax.shift_right_logical(local[...], 3), nn(chi, chot[...]) + nn(clo, chot[...]), 0.0
     )
     found = found[0:32] + found[32:64] + found[64:96] + found[96:128]
-    mask = (iota((8, E), 0) == child[...]).astype(f32)
-    pm = prolong[...].reshape(80, NN)
-    pm40 = jnp.concatenate([pm, jnp.zeros((80, 5), f32)], axis=1)
-    ph, pw = split(pm40)
-    pm3 = jnp.concatenate([ph, ph, pw], axis=0)
     fine = []
     for p in range(3):
         z = jnp.concatenate([mask * found[p * 10 + k:p * 10 + k + 1, :] for k in range(10)], axis=0)
@@ -328,7 +343,6 @@
         store.start()
     fine_grad = (STEP * gb, STEP * tr * lam0, STEP * gm)
 
-    pm144 = lanes3(pm, 48)
     rst[30:31, :] = local[...].astype(f32)
     rst[31:32, :] = jnp.zeros((1, E), f32)
     for p in range(3):
@@ -425,6 +439,8 @@
             pltpu.VMEM((1024, E), bf16),
             pltpu.VMEM((NF, NN, E), f32),
             pltpu.VMEM((NF, NN, E), f32),
+            pltpu.VMEM((40, 192), bf16),
+            pltpu.VMEM((16, OWN), i32),
             pltpu.SemaphoreType.DMA((5,)),
             pltpu.SemaphoreType.DMA((5,)),
             pltpu.SemaphoreType.DMA((2,)),

time: 33.2 us -> 33 us (level)
  no operation moved by 1% of the time
where the time goes in v3:
time: 33 us; the launch traced here: 32.8 us
  Pallas kernels  32.2 us (98%)
  between operations  0.65 us (2%)
    pallas_call x1, Pallas kernels, body(): pl.pallas_call(kernel, out_shape=results, in_specs=[hbm] * len(ops), out_...  30.3 us
    pallas_call x1, Pallas kernels, body(): pl.pallas_call(place, out_shape=results, in_specs=[anywhere] * 3, out_spe...  1.9 us

profile of v3, /device:TPU:1, one launch (start us, length us, event | category | flops | bytes accessed | tf_op | source)
XLA Modules:
  0.0 32.8 jit_solution(11436584469276256016)
XLA Ops:
  0.6 30.3 %shard_map.220 = (f32[9,35,256]{2,1,0:T(8,128)}, f32[9,35,256]{2,1,0:T(8,128)}, f32[30,32]{1,0:T(8,128)}) custom-call(f32[9,35,256]{2,1,0:T(8,128)} %refs_0_.1, f32[9,35,256]{2,1,0:T(8,128)} %refs_1_.1, f32[9,35,256]{2,1,0:T(8,128)} %refs_2_.1, f32[3,35,256]{2,1,0:T(8,128)} %refs_3_.1, f32[9,256]{1,0:T(8,128)} %refs_4_.1, f32[3,4,256]{2,1,0:T(4,128)} %refs_5_.1, ...), custom_call_target="tpu_custom_call" | custom-call | tf_op jit(solution)/shard_map/pallas_call | solution.py:417
  30.9 1.9 %shard_map.221 = (f32[9,35,256]{2,1,0:T(8,128)}, f32[9,35,256]{2,1,0:T(8,128)}, f32[30,32]{1,0:T(8,128)}) custom-call(f32[9,35,256]{2,1,0:T(8,128)} %get-tuple-element.6.refs_0_, f32[9,35,256]{2,1,0:T(8,128)} %get-tuple-element.7.refs_1_, f32[30,32]{1,0:T(8,128)} %get-tuple-element.8.refs_2_), custom_call_target="tpu_custom_call" | custom-call | tf_op jit(solution)/shard_map/pallas_call | solution.py:453

commit v4 on v3

--- a/solution.py
+++ b/solution.py
@@ -17,6 +17,7 @@
 NF, NN, E, NW, ND = 9, 35, 256, 32, 128
 OWN, TAB = 1024, 1152
 ROWS = 27 * 16
+MOVED = (*range(384, 399), *range(400, 409))
 
 
 def tables():
@@ -105,7 +106,7 @@
     owner, local, child, neighbor, orient, send_face, pick, turn,
     out_d, out_a, out_h,
     tab, hot, dq, jump, hn, xl, fs, ltr, rst, c1,
-    tr_s, tr_r, ag_s, ag_r, p1, p2, p3, chot, new_d, new_a, lmat, order,
+    tr_s, tr_r, ag_s, ag_r, p1, p2, p3, chot, new_d, new_a, lmat, order, packed, left,
     ssem, rsem, osem,
 ):
     region, wave = lax.axis_index("region"), lax.axis_index("wave")
@@ -166,11 +167,22 @@
                 tab[0, sc * 16:(sc + 1) * 16, span] = got[120 + f * 16:136 + f * 16].astype(bf16)
                 tab[1, sc * 16:(sc + 1) * 16, span] = got[184 + f * 16:200 + f * 16].astype(bf16)
 
-    pickt = (iota((OWN, 128), 0) == send_face[...]).astype(f32).astype(bf16)
-    sent = nn(tab[0, :, 0:OWN], pickt) + nn(tab[1, :, 0:OWN], pickt)
-    sent = below(sent, 512)
-    for j in range(4):
-        tr_s.reshape(4, 128, 128)[j] = sent[j * 128:(j + 1) * 128].T
+    turned = iota((8, 128), 1)
+    turned = (turned & 31) * 4 + lax.shift_right_logical(turned, 5)
+    chosen = jnp.broadcast_to(send_face[...].astype(f32), (8, 128))
+    chosen = jnp.take_along_axis(chosen, turned, axis=1, mode="promise_in_bounds").astype(i32)
+    pickt = (iota((OWN, 128), 0) == chosen[0:1]).astype(f32).astype(bf16)
+    packed[...] = nn(tab[0, :, 0:OWN], pickt) + nn(tab[1, :, 0:OWN], pickt)
+    for block, row in enumerate(MOVED):
+        packed[block * 16 + 15:block * 16 + 16, :] = packed[row:row + 1, :]
+    left[0:6, :] = packed[409:415, :]
+    left[6:21, :] = packed[416:431, :]
+    left[21:32, :] = jnp.zeros((11, 128), f32)
+    rows_s = tr_s.reshape(13, NW, 128)
+    for j in range(3):
+        rows_s[j * 4:j * 4 + 4] = packed[j * 128:(j + 1) * 128, :].T.reshape(4, NW, 128)
+    last = left[...].T
+    rows_s[12] = jnp.concatenate([last[c * 32:(c + 1) * 32] for c in range(4)], axis=1)
 
     pl.semaphore_wait(barrier, 79)
 
@@ -183,7 +195,9 @@
     tr_r[:, pl.ds(wave, 1)] = tr_s[:, pl.ds(wave, 1)]
 
     for f in range(4):
-        row = neighbor[f:f + 1, :].astype(i16)
+        named = neighbor[f:f + 1, :]
+        far = OWN + (named & 3) * 32 + lax.shift_right_logical(named - OWN, 2)
+        row = jnp.where(named < OWN, named, far).astype(i16)
         hot[:, f * E:(f + 1) * E] = jnp.where(
             iota((TAB, E), 0, i16) == row, jnp.ones((), bf16), jnp.zeros((), bf16)
         )
@@ -237,11 +251,20 @@
     pm144 = lanes3(pm, 48)
 
     wait(tr_r.at[:, pl.ds(0, NW - 1)], rsem.at[0])
-    for j in range(4):
-        rows = min(128, ROWS - j * 128)
-        hi, lo = split(tr_r.reshape(4, 128, 128)[j].T[0:rows])
-        tab[0, j * 128:j * 128 + rows, OWN:TAB] = hi
-        tab[1, j * 128:j * 128 + rows, OWN:TAB] = lo
+    rows_r = tr_r.reshape(13, NW, 128)
+    for j in range(3):
+        packed[j * 128:(j + 1) * 128, :] = rows_r[j * 4:j * 4 + 4].reshape(128, 128).T
+    last = rows_r[12]
+    left[...] = jnp.concatenate([last[:, c * 32:(c + 1) * 32] for c in range(4)], axis=0).T
+    for row in (399, 415, 431):
+        packed[row:row + 1, :] = jnp.zeros((1, 128), f32)
+    for block, row in enumerate(MOVED):
+        packed[row:row + 1, :] = packed[block * 16 + 15:block * 16 + 16, :]
+    packed[409:415, :] = left[0:6, :]
+    packed[416:431, :] = left[6:21, :]
+    hi, lo = split(packed[...])
+    tab[0, :, OWN:TAB] = hi
+    tab[1, :, OWN:TAB] = lo
     for f in range(4):
         span = slice(f * E, (f + 1) * E)
         jump[:, span] += nn(tab[0, :, OWN:TAB], hot[OWN:TAB, span]) + nn(tab[1, :, OWN:TAB], hot[OWN:TAB, span])
@@ -262,6 +285,9 @@
                 jump[sc * 16 + t * 8:sc * 16 + t * 8 + 8, span] = (
                     jnp.where(low[t * 8:t * 8 + 8], ga, gb) - own[t * 8:t * 8 + 8]
                 )
+
+    wait(ag_r.at[pl.ds(0, 63), 0], rsem.at[1])
+    send(ag_r.at[:, pl.ds(core, 1)], ag_r.at[:, pl.ds(core, 1)], 2, sibling)
 
     def terms(s):
         for f in range(4):
@@ -285,9 +311,6 @@
                 fs[s, at] = nn(lmat[...], xl[at])
 
     terms(0)
-
-    wait(ag_r.at[pl.ds(0, 63), 0], rsem.at[1])
-    send(ag_r.at[:, pl.ds(core, 1)], ag_r.at[:, pl.ds(core, 1)], 2, sibling)
 
     terms(1)
     terms(2)
@@ -431,8 +454,8 @@
             pltpu.VMEM((64, 128), f32),
             pltpu.VMEM((32, E), f32),
             pltpu.VMEM((248, 144), bf16),
-            pltpu.VMEM((4, NW, 4, 128), f32),
-            pltpu.VMEM((4, NW, 4, 128), f32),
+            pltpu.VMEM((13, NW, 1, 128), f32),
+            pltpu.VMEM((13, NW, 1, 128), f32),
             pltpu.VMEM((8, 128), f32),
             pltpu.VMEM((64, 2, 8, 128), f32),
             row, row, row,
@@ -441,6 +464,8 @@
             pltpu.VMEM((NF, NN, E), f32),
             pltpu.VMEM((40, 192), bf16),
             pltpu.VMEM((16, OWN), i32),
+            pltpu.VMEM((ROWS, 128), f32),
+            pltpu.VMEM((32, 128), f32),
             pltpu.SemaphoreType.DMA((5,)),
             pltpu.SemaphoreType.DMA((5,)),
             pltpu.SemaphoreType.DMA((2,)),

time: 33 us -> 32.2 us (0.976)
  Pallas kernels: 32.2 us -> 31.4 us
    pallas_call x1, Pallas kernels: 30.3 us -> 29.5 us  [body(): pl.pallas_call(kernel, out_shape=results, in_specs=[hbm] * len(ops), out_...]
where the time goes in v4:
time: 32.2 us; the launch traced here: 32 us
  Pallas kernels  31.4 us (98%)
  between operations  0.65 us (2%)
    pallas_call x1, Pallas kernels, body(): pl.pallas_call(kernel, out_shape=results, in_specs=[hbm] * len(ops), out_...  29.5 us
    pallas_call x1, Pallas kernels, body(): pl.pallas_call(place, out_shape=results, in_specs=[anywhere] * 3, out_spe...  1.9 us

profile of v4, /device:TPU:1, one launch (start us, length us, event | category | flops | bytes accessed | tf_op | source)
XLA Modules:
  0.0 32.0 jit_solution(12497390675750861773)
XLA Ops:
  0.6 29.5 %shard_map.220 = (f32[9,35,256]{2,1,0:T(8,128)}, f32[9,35,256]{2,1,0:T(8,128)}, f32[30,32]{1,0:T(8,128)}) custom-call(f32[9,35,256]{2,1,0:T(8,128)} %refs_0_.1, f32[9,35,256]{2,1,0:T(8,128)} %refs_1_.1, f32[9,35,256]{2,1,0:T(8,128)} %refs_2_.1, f32[3,35,256]{2,1,0:T(8,128)} %refs_3_.1, f32[9,256]{1,0:T(8,128)} %refs_4_.1, f32[3,4,256]{2,1,0:T(4,128)} %refs_5_.1, ...), custom_call_target="tpu_custom_call" | custom-call | tf_op jit(solution)/shard_map/pallas_call | solution.py:440
  30.1 1.9 %shard_map.221 = (f32[9,35,256]{2,1,0:T(8,128)}, f32[9,35,256]{2,1,0:T(8,128)}, f32[30,32]{1,0:T(8,128)}) custom-call(f32[9,35,256]{2,1,0:T(8,128)} %get-tuple-element.6.refs_0_, f32[9,35,256]{2,1,0:T(8,128)} %get-tuple-element.7.refs_1_, f32[30,32]{1,0:T(8,128)} %get-tuple-element.8.refs_2_), custom_call_target="tpu_custom_call" | custom-call | tf_op jit(solution)/shard_map/pallas_call | solution.py:478

commit v5 on v4

--- a/solution.py
+++ b/solution.py
@@ -129,9 +129,18 @@
 
         lax.fori_loop(low, high, one, 0)
 
+    half = lax.div(wave, 2)
+
+    def level(i):
+        return (region, lax.rem(wave + 2 * i, NW))
+
+    def across(i):
+        return (lax.rem(region + i, 4), wave)
+
     sibling = (region, wave + 1 - 2 * core)
     each(0, 16, lambda i: greet((region, lax.rem(wave + 2 * i + 1, NW))))
-    each(1, 64, lambda i: greet(alike(i)[1]))
+    each(1, 16, lambda i: greet(level(i)))
+    each(1, 4, lambda i: greet(across(i)))
 
     def send(src, dst, at, there):
         pltpu.make_async_remote_copy(
@@ -147,7 +156,7 @@
     cs = jnp.concatenate([coarse[...], jnp.zeros((2, 32), f32)], axis=0)
     cst = jnp.concatenate([cs, jnp.zeros((32, 96), f32)], axis=1).T
     ag_s[...] = jnp.concatenate([cst[q * 8:q * 8 + 8, 0:32] for q in range(4)], axis=1)
-    ag_r[pl.ds(chip, 1), pl.ds(core, 1)] = ag_s[...].reshape(1, 1, 8, 128)
+    ag_r[pl.ds(half, 1), pl.ds(core, 1), pl.ds(region, 1)] = ag_s[...].reshape(1, 1, 1, 8, 128)
 
     u = (iota((ND, E), 0) == owner[...]).astype(f32).astype(bf16)
     ub = u.astype(f32)
@@ -184,14 +193,14 @@
     last = left[...].T
     rows_s[12] = jnp.concatenate([last[c * 32:(c + 1) * 32] for c in range(4)], axis=1)
 
-    pl.semaphore_wait(barrier, 79)
+    pl.semaphore_wait(barrier, 34)
+    each(1, 4, lambda i: send(ag_s, ag_r.at[half, core, region], 1, across(i)))
 
     def send_trace(i):
         w = lax.rem(wave + i, NW)
         send(tr_s.at[:, pl.ds(w, 1)], tr_r.at[:, pl.ds(wave, 1)], 0, (region, w))
 
     each(1, NW, send_trace)
-    each(1, 64, lambda i: send(ag_s, ag_r.at[chip, core], 1, alike(i)[1]))
     tr_r[:, pl.ds(wave, 1)] = tr_s[:, pl.ds(wave, 1)]
 
     for f in range(4):
@@ -202,7 +211,11 @@
             iota((TAB, E), 0, i16) == row, jnp.ones((), bf16), jnp.zeros((), bf16)
         )
 
-    line = (owner[...] * 8 + (local[...] & 7)).astype(i16)
+    wait(ag_r.at[0, 0, pl.ds(0, 3)], rsem.at[1])
+    each(1, 16, lambda i: send(ag_r.at[half, core], ag_r.at[half, core], 5, level(i)))
+
+    line = ((owner[...] & 31) * 4 + lax.shift_right_logical(owner[...], 5)) * 8
+    line = (line + (local[...] & 7)).astype(i16)
     chot[...] = jnp.where(iota((1024, E), 0, i16) == line, jnp.ones((), bf16), jnp.zeros((), bf16))
 
     for f in range(4):
@@ -286,7 +299,7 @@
                     jnp.where(low[t * 8:t * 8 + 8], ga, gb) - own[t * 8:t * 8 + 8]
                 )
 
-    wait(ag_r.at[pl.ds(0, 63), 0], rsem.at[1])
+    wait(ag_r.at[pl.ds(0, 15), 0], rsem.at[5])
     send(ag_r.at[:, pl.ds(core, 1)], ag_r.at[:, pl.ds(core, 1)], 2, sibling)
 
     def terms(s):
@@ -315,6 +328,23 @@
     terms(1)
     terms(2)
 
+    m0, m1, m2 = (below(model[p], 40) for p in range(3))
+
+    def lam(s):
+        return fs[s, 3] + fs[s, 4] + fs[s, 5]
+
+    def mu(s, k):
+        return 2.0 * fs[s, 3 + k] if k < 3 else fs[s, 3 + k]
+
+    for s, ref in ((1, dl), (2, ad)):
+        lams = m1 * lam(s)
+        for c in range(NF):
+            grown = m0 * fs[s, c] if c < 3 else m2 * mu(s, c - 3)
+            if 3 <= c < 6:
+                grown = grown + lams
+            fs[s, 9 + c] = below(ref[c], 40) + STEP * (grown + fs[s, 9 + c])
+    lam0 = lam(0)
+
     wait(ag_r.at[:, pl.ds(0, 1)], rsem.at[2])
     chi, clo = split(ag_r[...].reshape(1024, 128).T)
     found = jnp.where(
@@ -326,39 +356,29 @@
         z = jnp.concatenate([mask * found[p * 10 + k:p * 10 + k + 1, :] for k in range(10)], axis=0)
         fine.append(tn(pm3, rows3(z)))
 
-    m0, m1, m2 = (below(model[p], 40) for p in range(3))
-
-    def lam(s):
-        return fs[s, 3] + fs[s, 4] + fs[s, 5]
-
-    def mu(s, k):
-        return 2.0 * fs[s, 3 + k] if k < 3 else fs[s, 3 + k]
-
-    lam0 = lam(0)
-    lam1 = m1 * lam(1) + fine[1] * lam0
-    lam2 = m1 * lam(2)
-    obs = below(observe[...], 40)
+    obs = STEP * below(observe[...], 40)
+    fine = [STEP * x for x in fine]
+    lam1 = fine[1] * lam0
     gb = jnp.zeros((40, E), f32)
     tr = jnp.zeros((40, E), f32)
     gm = jnp.zeros((40, E), f32)
     for c in range(NF):
         if c < 3:
-            wave_d = m0 * fs[1, c] + fine[0] * fs[0, c]
-            wave_a = m0 * fs[2, c]
+            term = fs[0, c]
+            nd = fs[1, 9 + c] + fine[0] * term
         else:
-            wave_d = m2 * mu(1, c - 3) + fine[2] * mu(0, c - 3)
-            wave_a = m2 * mu(2, c - 3)
+            term = mu(0, c - 3)
+            more = fine[2] * term
             if c < 6:
-                wave_d = wave_d + lam1
-                wave_a = wave_a + lam2
-        nd = below(dl[c], 40) + STEP * (wave_d + fs[1, 9 + c])
-        na = below(ad[c], 40) + STEP * (wave_a + fs[2, 9 + c] + obs * nd)
+                more = more + lam1
+            nd = fs[1, 9 + c] + more
+        na = fs[2, 9 + c] + obs * nd
         new_d[c] = nd[0:NN]
         new_a[c] = na[0:NN]
         if c < 3:
-            gb = gb + na * fs[0, c]
+            gb = gb + na * term
         else:
-            gm = gm + na * mu(0, c - 3)
+            gm = gm + na * term
             if c < 6:
                 tr = tr + na
     stores = [pltpu.make_async_copy(new_d, out_d, osem.at[0]), pltpu.make_async_copy(new_a, out_a, osem.at[1])]
@@ -396,7 +416,8 @@
     out_h[...] = total[0:30] + reg[...] * coarse[...]
 
     wait(tr_s.at[:, pl.ds(0, NW - 1)], ssem.at[0])
-    wait(ag_r.at[pl.ds(0, 63), 0], ssem.at[1])
+    wait(ag_r.at[0, 0, pl.ds(0, 3)], ssem.at[1])
+    wait(ag_r.at[pl.ds(0, 15), 0], ssem.at[5])
     wait(ag_r.at[:, pl.ds(0, 1)], ssem.at[2])
     wait(p1.at[:, pl.ds(0, 1)], ssem.at[3])
     wait(p2.at[pl.ds(0, 63)], ssem.at[4])
@@ -457,7 +478,7 @@
             pltpu.VMEM((13, NW, 1, 128), f32),
             pltpu.VMEM((13, NW, 1, 128), f32),
             pltpu.VMEM((8, 128), f32),
-            pltpu.VMEM((64, 2, 8, 128), f32),
+            pltpu.VMEM((16, 2, 4, 8, 128), f32),
             row, row, row,
             pltpu.VMEM((1024, E), bf16),
             pltpu.VMEM((NF, NN, E), f32),
@@ -466,8 +487,8 @@
             pltpu.VMEM((16, OWN), i32),
             pltpu.VMEM((ROWS, 128), f32),
             pltpu.VMEM((32, 128), f32),
-            pltpu.SemaphoreType.DMA((5,)),
-            pltpu.SemaphoreType.DMA((5,)),
+            pltpu.SemaphoreType.DMA((6,)),
+            pltpu.SemaphoreType.DMA((6,)),
             pltpu.SemaphoreType.DMA((2,)),
             pltpu.SemaphoreType.DMA((N_OPS,)),
         ],

time: 32.2 us -> 31 us (0.963)
  Pallas kernels: 31.4 us -> 30.2 us
    pallas_call x1, Pallas kernels: 29.5 us -> 28.3 us  [body(): pl.pallas_call(kernel, out_shape=results, in_specs=[hbm] * len(ops), out_...]
where the time goes in v5:
time: 31 us; the launch traced here: 30.9 us
  Pallas kernels  30.2 us (97%)
  between operations  0.65 us (2%)
    pallas_call x1, Pallas kernels, body(): pl.pallas_call(kernel, out_shape=results, in_specs=[hbm] * len(ops), out_...  28.3 us
    pallas_call x1, Pallas kernels, body(): pl.pallas_call(place, out_shape=results, in_specs=[anywhere] * 3, out_spe...  1.9 us

profile of v5, /device:TPU:1, one launch (start us, length us, event | category | flops | bytes accessed | tf_op | source)
XLA Modules:
  0.0 30.9 jit_solution(7257956747238222692)
XLA Ops:
  0.6 28.3 %shard_map.220 = (f32[9,35,256]{2,1,0:T(8,128)}, f32[9,35,256]{2,1,0:T(8,128)}, f32[30,32]{1,0:T(8,128)}) custom-call(f32[9,35,256]{2,1,0:T(8,128)} %refs_0_.1, f32[9,35,256]{2,1,0:T(8,128)} %refs_1_.1, f32[9,35,256]{2,1,0:T(8,128)} %refs_2_.1, f32[3,35,256]{2,1,0:T(8,128)} %refs_3_.1, f32[9,256]{1,0:T(8,128)} %refs_4_.1, f32[3,4,256]{2,1,0:T(4,128)} %refs_5_.1, ...), custom_call_target="tpu_custom_call" | custom-call | tf_op jit(solution)/shard_map/pallas_call | solution.py:461
  29.0 1.9 %shard_map.221 = (f32[9,35,256]{2,1,0:T(8,128)}, f32[9,35,256]{2,1,0:T(8,128)}, f32[30,32]{1,0:T(8,128)}) custom-call(f32[9,35,256]{2,1,0:T(8,128)} %get-tuple-element.6.refs_0_, f32[9,35,256]{2,1,0:T(8,128)} %get-tuple-element.7.refs_1_, f32[30,32]{1,0:T(8,128)} %get-tuple-element.8.refs_2_), custom_call_target="tpu_custom_call" | custom-call | tf_op jit(solution)/shard_map/pallas_call | solution.py:499

commit v6 on v5

--- a/solution.py
+++ b/solution.py
@@ -106,21 +106,16 @@
     owner, local, child, neighbor, orient, send_face, pick, turn,
     out_d, out_a, out_h,
     tab, hot, dq, jump, hn, xl, fs, ltr, rst, c1,
-    tr_s, tr_r, ag_s, ag_r, p1, p2, p3, chot, new_d, new_a, lmat, order, packed, left,
+    tr_s, tr_r, ag_s, ag_r, p1, p3, chot, new_d, new_a, lmat, order, packed, left,
     ssem, rsem, osem,
 ):
     region, wave = lax.axis_index("region"), lax.axis_index("wave")
     me = region * NW + wave
     core = lax.rem(wave, 2)
-    chip = lax.div(me, 2)
     barrier = pltpu.get_barrier_semaphore()
 
     def greet(there):
         pl.semaphore_signal(barrier, inc=1, device_id=there, device_id_type=MESH)
-
-    def alike(i):
-        d = lax.rem(me + 2 * i, ND)
-        return lax.div(d, 2), (lax.div(d, NW), lax.rem(d, NW))
 
     def each(low, high, act):
         def one(i, c):
@@ -212,7 +207,7 @@
         )
 
     wait(ag_r.at[0, 0, pl.ds(0, 3)], rsem.at[1])
-    each(1, 16, lambda i: send(ag_r.at[half, core], ag_r.at[half, core], 5, level(i)))
+    each(1, 16, lambda i: send(ag_r.at[half, core], ag_r.at[half, core], 4, level(i)))
 
     line = ((owner[...] & 31) * 4 + lax.shift_right_logical(owner[...], 5)) * 8
     line = (line + (local[...] & 7)).astype(i16)
@@ -298,9 +293,6 @@
                 jump[sc * 16 + t * 8:sc * 16 + t * 8 + 8, span] = (
                     jnp.where(low[t * 8:t * 8 + 8], ga, gb) - own[t * 8:t * 8 + 8]
                 )
-
-    wait(ag_r.at[pl.ds(0, 15), 0], rsem.at[5])
-    send(ag_r.at[:, pl.ds(core, 1)], ag_r.at[:, pl.ds(core, 1)], 2, sibling)
 
     def terms(s):
         for f in range(4):
@@ -324,6 +316,9 @@
                 fs[s, at] = nn(lmat[...], xl[at])
 
     terms(0)
+
+    wait(ag_r.at[pl.ds(0, 15), 0], rsem.at[4])
+    send(ag_r.at[:, pl.ds(core, 1)], ag_r.at[:, pl.ds(core, 1)], 2, sibling)
 
     terms(1)
     terms(2)
@@ -394,17 +389,14 @@
     slot = lax.div(iota((128, E), 0), 32) == before
     wh, wl = split(jnp.where(slot, jnp.concatenate([rst[...]] * 4, axis=0), 0.0))
     p1.reshape(ND, 128)[...] = nt(u, wh) + nt(u, wl)
-    send(p1.at[:, pl.ds(1 - core, 1)], p2.at[:, pl.ds(core, 1)], 3, sibling)
-    p2[:, pl.ds(core, 1)] = p1[:, pl.ds(core, 1)]
-    wait(p2.at[:, pl.ds(0, 1)], rsem.at[3])
 
     def send_partial(i):
-        to, there = alike(i)
-        send(p2.at[to], p3.at[chip], 4, there)
-
-    each(1, 64, send_partial)
-    p3[pl.ds(chip, 1)] = p2[pl.ds(chip, 1)]
-    wait(p3.at[pl.ds(0, 63)], rsem.at[4])
+        d = lax.rem(me + i, ND)
+        send(p1.at[d], p3.at[me], 3, (lax.div(d, NW), lax.rem(d, NW)))
+
+    each(1, ND, send_partial)
+    p3[pl.ds(me, 1)] = p1[pl.ds(me, 1)]
+    wait(p3.at[pl.ds(0, ND - 1)], rsem.at[3])
     gh, gl = split(p3.reshape(ND, 128)[...])
     place_of = lax.rem(iota((128, 128), 1), 32)
     spread = (iota((128, 128), 0) == iota((128, 128), 1) - place_of + 30).astype(f32).astype(bf16)
@@ -417,10 +409,9 @@
 
     wait(tr_s.at[:, pl.ds(0, NW - 1)], ssem.at[0])
     wait(ag_r.at[0, 0, pl.ds(0, 3)], ssem.at[1])
-    wait(ag_r.at[pl.ds(0, 15), 0], ssem.at[5])
+    wait(ag_r.at[pl.ds(0, 15), 0], ssem.at[4])
     wait(ag_r.at[:, pl.ds(0, 1)], ssem.at[2])
-    wait(p1.at[:, pl.ds(0, 1)], ssem.at[3])
-    wait(p2.at[pl.ds(0, 63)], ssem.at[4])
+    wait(p1.at[pl.ds(0, ND - 1)], ssem.at[3])
     for store in stores:
         store.wait()
 
@@ -452,7 +443,7 @@
     vmem = pl.BlockSpec(memory_space=pltpu.VMEM)
     anywhere = pl.BlockSpec(memory_space=pl.ANY)
     hbm = pl.BlockSpec(memory_space=pltpu.HBM)
-    row = pltpu.VMEM((64, 2, 1, 128), f32)
+    row = pltpu.VMEM((ND, 1, 128), f32)
     results = (
         jax.ShapeDtypeStruct((NF, NN, E), f32),
         jax.ShapeDtypeStruct((NF, NN, E), f32),
@@ -479,7 +470,7 @@
             pltpu.VMEM((13, NW, 1, 128), f32),
             pltpu.VMEM((8, 128), f32),
             pltpu.VMEM((16, 2, 4, 8, 128), f32),
-            row, row, row,
+            row, row,
             pltpu.VMEM((1024, E), bf16),
             pltpu.VMEM((NF, NN, E), f32),
             pltpu.VMEM((NF, NN, E), f32),
@@ -487,8 +478,8 @@
             pltpu.VMEM((16, OWN), i32),
             pltpu.VMEM((ROWS, 128), f32),
             pltpu.VMEM((32, 128), f32),
-            pltpu.SemaphoreType.DMA((6,)),
-            pltpu.SemaphoreType.DMA((6,)),
+            pltpu.SemaphoreType.DMA((5,)),
+            pltpu.SemaphoreType.DMA((5,)),
             pltpu.SemaphoreType.DMA((2,)),
             pltpu.SemaphoreType.DMA((N_OPS,)),
         ],

time: 31 us -> 30.4 us (0.981)
  Pallas kernels: 30.2 us -> 29.6 us
    pallas_call x1, Pallas kernels: 28.3 us -> 27.7 us  [body(): pl.pallas_call(kernel, out_shape=results, in_specs=[hbm] * len(ops), out_...]
where the time goes in v6:
time: 30.4 us; the launch traced here: 30.2 us
  Pallas kernels  29.6 us (97%)
  between operations  0.65 us (2%)
    pallas_call x1, Pallas kernels, body(): pl.pallas_call(kernel, out_shape=results, in_specs=[hbm] * len(ops), out_...  27.7 us
    pallas_call x1, Pallas kernels, body(): pl.pallas_call(place, out_shape=results, in_specs=[anywhere] * 3, out_spe...  1.9 us

profile of v6, /device:TPU:1, one launch (start us, length us, event | category | flops | bytes accessed | tf_op | source)
XLA Modules:
  0.0 30.2 jit_solution(18012087872910026812)
XLA Ops:
  0.6 27.7 %shard_map.220 = (f32[9,35,256]{2,1,0:T(8,128)}, f32[9,35,256]{2,1,0:T(8,128)}, f32[30,32]{1,0:T(8,128)}) custom-call(f32[9,35,256]{2,1,0:T(8,128)} %refs_0_.1, f32[9,35,256]{2,1,0:T(8,128)} %refs_1_.1, f32[9,35,256]{2,1,0:T(8,128)} %refs_2_.1, f32[3,35,256]{2,1,0:T(8,128)} %refs_3_.1, f32[9,256]{1,0:T(8,128)} %refs_4_.1, f32[3,4,256]{2,1,0:T(4,128)} %refs_5_.1, ...), custom_call_target="tpu_custom_call" | custom-call | tf_op jit(solution)/shard_map/pallas_call | solution.py:452
  28.3 1.9 %shard_map.221 = (f32[9,35,256]{2,1,0:T(8,128)}, f32[9,35,256]{2,1,0:T(8,128)}, f32[30,32]{1,0:T(8,128)}) custom-call(f32[9,35,256]{2,1,0:T(8,128)} %get-tuple-element.6.refs_0_, f32[9,35,256]{2,1,0:T(8,128)} %get-tuple-element.7.refs_1_, f32[30,32]{1,0:T(8,128)} %get-tuple-element.8.refs_2_), custom_call_target="tpu_custom_call" | custom-call | tf_op jit(solution)/shard_map/pallas_call | solution.py:490

commit v7 on v6

--- a/solution.py
+++ b/solution.py
@@ -209,9 +209,11 @@
     wait(ag_r.at[0, 0, pl.ds(0, 3)], rsem.at[1])
     each(1, 16, lambda i: send(ag_r.at[half, core], ag_r.at[half, core], 4, level(i)))
 
-    line = ((owner[...] & 31) * 4 + lax.shift_right_logical(owner[...], 5)) * 8
-    line = (line + (local[...] & 7)).astype(i16)
-    chot[...] = jnp.where(iota((1024, E), 0, i16) == line, jnp.ones((), bf16), jnp.zeros((), bf16))
+    line = (lax.shift_right_logical(owner[...] & 31, 1) * 4 + lax.shift_right_logical(owner[...], 5)) * 8
+    line = line + (local[...] & 7)
+    for k in range(2):
+        row = jnp.where((owner[...] & 1) == (core + k - 2 * core * k), line, -1).astype(i16)
+        chot[k] = jnp.where(iota((512, E), 0, i16) == row, jnp.ones((), bf16), jnp.zeros((), bf16))
 
     for f in range(4):
         span = slice(f * E, (f + 1) * E)
@@ -320,6 +322,12 @@
     wait(ag_r.at[pl.ds(0, 15), 0], rsem.at[4])
     send(ag_r.at[:, pl.ds(core, 1)], ag_r.at[:, pl.ds(core, 1)], 2, sibling)
 
+    def looked_up(k, at):
+        hi, lo = split(ag_r[:, pl.ds(at, 1)].reshape(512, 128).T)
+        return nn(hi, chot[k]) + nn(lo, chot[k])
+
+    near = looked_up(0, core)
+
     terms(1)
     terms(2)
 
@@ -341,9 +349,8 @@
     lam0 = lam(0)
 
     wait(ag_r.at[:, pl.ds(0, 1)], rsem.at[2])
-    chi, clo = split(ag_r[...].reshape(1024, 128).T)
     found = jnp.where(
-        lax.div(iota((128, E), 0), 32) == lax.shift_right_logical(local[...], 3), nn(chi, chot[...]) + nn(clo, chot[...]), 0.0
+        lax.div(iota((128, E), 0), 32) == lax.shift_right_logical(local[...], 3), near + looked_up(1, 1 - core), 0.0
     )
     found = found[0:32] + found[32:64] + found[64:96] + found[96:128]
     fine = []
@@ -396,16 +403,17 @@
 
     each(1, ND, send_partial)
     p3[pl.ds(me, 1)] = p1[pl.ds(me, 1)]
+    place_of = lax.rem(iota((128, 128), 1), 32)
+    spread = (iota((128, 128), 0) == iota((128, 128), 1) - place_of + 30).astype(f32).astype(bf16)
+    same = lax.div(iota((128, 128), 0), 32) == lax.div(iota((128, 128), 1), 32)
+    kept = reg[...] * coarse[...]
     wait(p3.at[pl.ds(0, ND - 1)], rsem.at[3])
     gh, gl = split(p3.reshape(ND, 128)[...])
-    place_of = lax.rem(iota((128, 128), 1), 32)
-    spread = (iota((128, 128), 0) == iota((128, 128), 1) - place_of + 30).astype(f32).astype(bf16)
     asked = (nn(gh, spread).astype(i32) == place_of).astype(f32).astype(bf16)
-    same = lax.div(iota((128, 128), 0), 32) == lax.div(iota((128, 128), 1), 32)
     total = jnp.where(same, tn(gh, asked) + tn(gl, asked), 0.0)
     total = total[0:32] + total[32:64] + total[64:96] + total[96:128]
     total = total[:, 0:32] + total[:, 32:64] + total[:, 64:96] + total[:, 96:128]
-    out_h[...] = total[0:30] + reg[...] * coarse[...]
+    out_h[...] = total[0:30] + kept
 
     wait(tr_s.at[:, pl.ds(0, NW - 1)], ssem.at[0])
     wait(ag_r.at[0, 0, pl.ds(0, 3)], ssem.at[1])
@@ -471,7 +479,7 @@
             pltpu.VMEM((8, 128), f32),
             pltpu.VMEM((16, 2, 4, 8, 128), f32),
             row, row,
-            pltpu.VMEM((1024, E), bf16),
+            pltpu.VMEM((2, 512, E), bf16),
             pltpu.VMEM((NF, NN, E), f32),
             pltpu.VMEM((NF, NN, E), f32),
             pltpu.VMEM((40, 192), bf16),

time: 30.4 us -> 30.4 us (level)
  no operation moved by 1% of the time
where the time goes in v7:
time: 30.4 us; the launch traced here: 30.3 us
  Pallas kernels  29.6 us (97%)
  between operations  0.65 us (2%)
    pallas_call x1, Pallas kernels, body(): pl.pallas_call(kernel, out_shape=results, in_specs=[hbm] * len(ops), out_...  27.7 us
    pallas_call x1, Pallas kernels, body(): pl.pallas_call(place, out_shape=results, in_specs=[anywhere] * 3, out_spe...  1.9 us

profile of v7, /device:TPU:1, one launch (start us, length us, event | category | flops | bytes accessed | tf_op | source)
XLA Modules:
  0.0 30.3 jit_solution(17127283851876702210)
XLA Ops:
  0.6 27.7 %shard_map.220 = (f32[9,35,256]{2,1,0:T(8,128)}, f32[9,35,256]{2,1,0:T(8,128)}, f32[30,32]{1,0:T(8,128)}) custom-call(f32[9,35,256]{2,1,0:T(8,128)} %refs_0_.1, f32[9,35,256]{2,1,0:T(8,128)} %refs_1_.1, f32[9,35,256]{2,1,0:T(8,128)} %refs_2_.1, f32[3,35,256]{2,1,0:T(8,128)} %refs_3_.1, f32[9,256]{1,0:T(8,128)} %refs_4_.1, f32[3,4,256]{2,1,0:T(4,128)} %refs_5_.1, ...), custom_call_target="tpu_custom_call" | custom-call | tf_op jit(solution)/shard_map/pallas_call | solution.py:460
  28.4 1.9 %shard_map.221 = (f32[9,35,256]{2,1,0:T(8,128)}, f32[9,35,256]{2,1,0:T(8,128)}, f32[30,32]{1,0:T(8,128)}) custom-call(f32[9,35,256]{2,1,0:T(8,128)} %get-tuple-element.6.refs_0_, f32[9,35,256]{2,1,0:T(8,128)} %get-tuple-element.7.refs_1_, f32[30,32]{1,0:T(8,128)} %get-tuple-element.8.refs_2_), custom_call_target="tpu_custom_call" | custom-call | tf_op jit(solution)/shard_map/pallas_call | solution.py:498
